TPU v7x, 256 devices: a whole 4x4x8 slice. The times are simulated.
256 devices in a mesh: row: 16 (over x, y), col: 16 (over z, core).
Axes of the slice: x: 4, y: 4, z: 8, core: 2. Of those that a mesh axis runs over, the one named last changes fastest.
Arguments:
- pan_left: bfloat16 [2, 16, 2048, 64], P(None, 'row', 'col')
- pan_right: bfloat16 [2, 16, 2048, 64], P(None, 'row', 'col')
- panel_rank: int32 [2, 16], P(None, 'row'), may hold values from 8 to 64, as said below
- diag_tiles: float32 [2, 16, 2048, 2048], P(None, 'row', 'col'), as said below
- col_right: bfloat16 [2, 16, 64, 2048], P(None, 'row', 'col'), may hold values from -6 to 6
- column_rank: int32 [2, 16], P(None, 'row'), may hold values from 8 to 64, as said below
Outputs:
- panel_update: bfloat16 [2, 16, 2, 16, 2048, 64], P(None, 'row', None, 'col')
- diag_new: float32 [2, 16, 2048, 2048], P(None, 'row', 'col')
- lead_factor: float32 [2048, 2048], P('row', 'col')
- col_solved: float32 [2, 16, 64, 2048], P(None, 'row', 'col')
Inputs may be any that keep to these rules, and one draw needn't show every extreme that they name: `panel_rank`: some tile has rank exactly 8 and some exactly 64. `column_rank`: some tile has rank exactly 8 and some exactly 64. `diag_tiles`: every tile is symmetric and diag_new for tile 0 is positive definite.
All inputs are finite; a program needn't handle non-finite values.
Results may differ from a plain program's by a relative error of at most 0.0049.
Values may be sent and summed in bfloat16 or wider, within the bound.
A program may use at most 128 MiB of HBM per device.

v0:
```python
import jax
import jax.numpy as jnp
from jax import lax
from jax.sharding import PartitionSpec as P


def spread(value, axis, source):
    kept = jnp.where(lax.axis_index(axis) == source, value, 0).astype(value.dtype)
    return lax.psum(kept, axis)


def blocked_cholesky(matrix):
    order = matrix.shape[0]
    step_rows = min(order, 512)
    count_steps = order // step_rows
    working = matrix
    factor_columns = []
    for position in range(count_steps):
        offset = position * step_rows
        diagonal_block = working[:step_rows, :step_rows]
        diagonal_factor = jnp.linalg.cholesky(diagonal_block)
        lower_block = working[step_rows:, :step_rows]
        lower_factor = lax.linalg.triangular_solve(
            diagonal_factor, lower_block, left_side=False, lower=True, transpose_a=True
        )
        upper_zeros = jnp.zeros((offset, step_rows), jnp.float32)
        factor_columns.append(jnp.concatenate([upper_zeros, diagonal_factor, lower_factor], axis=0))
        trailing = working[step_rows:, step_rows:]
        working = trailing - jnp.dot(
            lower_factor,
            lower_factor.T,
            precision=lax.Precision.HIGHEST,
            preferred_element_type=jnp.float32,
        )
    return jnp.concatenate(factor_columns, axis=1)


def blocked_forward(factor, right_side):
    order = factor.shape[0]
    step_rows = min(order, 512)
    count_steps = order // step_rows
    solved_parts = []
    for position in range(count_steps):
        offset = position * step_rows
        target = right_side[offset : offset + step_rows]
        if position > 0:
            earlier = jnp.concatenate(solved_parts, axis=0)
            coupling = factor[offset : offset + step_rows, :offset]
            target = target - jnp.dot(
                coupling,
                earlier,
                precision=lax.Precision.HIGHEST,
                preferred_element_type=jnp.float32,
            )
        diagonal_factor = factor[offset : offset + step_rows, offset : offset + step_rows]
        solved_parts.append(
            lax.linalg.triangular_solve(diagonal_factor, target, left_side=True, lower=True)
        )
    return jnp.concatenate(solved_parts, axis=0)


def body(pan_left, pan_right, panel_rank, diag_tiles, col_right, column_rank):
    tile_rows = pan_left.shape[0]
    slab_rows = pan_left.shape[2]
    rank_width = pan_left.shape[3]
    tile_order = diag_tiles.shape[3]
    row_count = lax.axis_size("row")
    col_count = lax.axis_size("col")
    row_index = lax.axis_index("row")
    col_index = lax.axis_index("col")
    col_tiles = tile_rows * row_count // col_count
    columns = lax.broadcasted_iota(jnp.int32, pan_left.shape, 3)
    keep_mask = columns < panel_rank[:, :, None, None]
    zeros_half = jnp.zeros_like(pan_left)
    left_masked = jnp.where(keep_mask, pan_left, zeros_half)
    right_masked = jnp.where(keep_mask, pan_right, zeros_half)
    left_full, right_full = (
        lax.all_gather(left_masked, "col", axis=2, tiled=True),
        lax.all_gather(right_masked, "col", axis=2, tiled=True),
    )
    left_tiles = left_full[:, 0]
    right_tiles = right_full[:, 0]
    own_gram = jnp.einsum(
        "anr,ans->ars", right_tiles, right_tiles, preferred_element_type=jnp.float32
    ).astype(jnp.bfloat16)
    all_tiles = lax.all_gather(right_full, "row", axis=1, tiled=True)
    theirs = lax.dynamic_index_in_dim(all_tiles, col_index, 1, keepdims=False)
    cross_sum = jnp.einsum("anr,bns->arbs", right_tiles, theirs, preferred_element_type=jnp.float32)
    cross_gram = cross_sum.astype(jnp.bfloat16)
    tile_update = jnp.einsum(
        "anr,arbs->abns", left_tiles, cross_gram, preferred_element_type=jnp.float32
    )
    row_ids = lax.broadcasted_iota(jnp.int32, (tile_rows, col_tiles), 0) * row_count + row_index
    col_ids = lax.broadcasted_iota(jnp.int32, (tile_rows, col_tiles), 1) * col_count + col_index
    lower_mask = (row_ids > col_ids)[:, :, None, None]
    panel_update = jnp.where(lower_mask, tile_update, jnp.zeros_like(tile_update)).astype(
        jnp.bfloat16
    )
    panel_update = panel_update.reshape(tile_rows, 1, col_tiles, 1, tile_order, rank_width)
    products = jnp.einsum(
        "anr,ars->ans", left_tiles, own_gram, preferred_element_type=jnp.float32
    ).astype(jnp.bfloat16)
    product_rows = lax.dynamic_slice_in_dim(products, col_index * slab_rows, slab_rows, 1)
    correction = jnp.einsum(
        "ans,ams->anm", product_rows, left_tiles, preferred_element_type=jnp.float32
    )
    diag_new = diag_tiles - correction[:, None]
    lead_source = diag_new[0, 0]
    lead_rows = spread(lead_source, "row", 0)
    lead_tile = lax.all_gather(lead_rows, "col", axis=0, tiled=True)
    lead_factor = blocked_cholesky(lead_tile)
    block_rows = tile_order // row_count
    block_cols = tile_order // col_count
    lead_part = lax.dynamic_slice(
        lead_factor, (row_index * block_rows, col_index * block_cols), (block_rows, block_cols)
    )
    narrow_rows = col_right.shape[2]
    rank_ids = lax.broadcasted_iota(jnp.int32, col_right.shape, 2) + col_index * narrow_rows
    tile_ids = lax.broadcasted_iota(jnp.int32, col_right.shape, 0) * row_count + row_index
    keep_right = (rank_ids < column_rank[:, :, None, None]) & (tile_ids >= 1)
    right_kept = jnp.where(keep_right, col_right, jnp.zeros_like(col_right))
    right_side = right_kept.astype(jnp.float32).reshape(-1, tile_order).T
    solution = blocked_forward(lead_factor, right_side)
    col_solved = solution.T.reshape(col_right.shape)
    return (panel_update, diag_new, lead_part, col_solved)


def solution(mesh):
    placed = (
        P(None, "row", "col", None),
        P(None, "row", "col", None),
        P(None, "row"),
        P(None, "row", "col", None),
        P(None, "row", "col", None),
        P(None, "row"),
    )
    return jax.shard_map(
        body,
        mesh=mesh,
        in_specs=placed,
        out_specs=(
            P(None, "row", None, "col", None, None),
            P(None, "row", "col", None),
            P("row", "col"),
            P(None, "row", "col", None),
        ),
        check_vma=False,
    )
```

profile of v0, /device:TPU:1, one launch (start us, length us, event | category | flops | bytes accessed | tf_op | source)
XLA Modules:
  0.0 1057.1 jit_solution(1739891476128516880)
XLA Ops:
  8.1 22.8 %all_gather.12 = bf16[2,1,2048,64]{2,3,0,1:T(8,128)(2,1)S(1)} all-gather(bf16[2,1,128,64]{2,3,0,1:T(8,128)(2,1)S(1)} %get-tuple-element.156), channel_id=1, replica_groups=mesh['row'=16,'col'=16] {'col'}, dimensions={2}, use_global_device_ids=true | all-gather | bytes 557056 | tf_op jit(solution)/shard_map/all_gather | solution.py:79
  30.8 15.9 %all_gather.14 = bf16[2,1,2048,64]{2,3,0,1:T(8,128)(2,1)S(1)} all-gather(bf16[2,1,128,64]{2,3,0,1:T(8,128)(2,1)S(1)} %get-tuple-element.157), channel_id=1, replica_groups=mesh['row'=16,'col'=16] {'col'}, dimensions={2}, use_global_device_ids=true | all-gather | bytes 557056 | tf_op jit(solution)/shard_map/all_gather | solution.py:78
  55.1 93.3 %all-reduce.4.cloned.1.call-done = f32[128,2048]{0,1:T(8,128)} async-done(((f32[128,2048]{0,1:T(8,128)}), f32[128,2048]{0,1:T(8,128)}) %all-reduce.4.cloned.1.call-update) | async-done | bytes 1048592 | tf_op jit(solution)/shard_map/psum | solution.py:9
  151.2 76.1 %all-gather.3.cloned.1.call-done = bf16[2,16,2048,64]{2,3,0,1:T(8,128)(2,1)} async-done(((bf16[2,1,2048,64]{2,3,0,1:T(8,128)(2,1)}), bf16[2,16,2048,64]{2,3,0,1:T(8,128)(2,1)}) %all-gather.3.cloned.1.call-update) | async-done | bytes 8388624 | tf_op jit(solution)/shard_map/all_gather | solution.py:86
  227.3 3.2 fusion.22
  230.5 101.6 %all-gather.5.cloned.1.call-done = f32[2048,2048]{0,1:T(8,128)} async-done(((f32[128,2048]{0,1:T(8,128)}), f32[2048,2048]{0,1:T(8,128)}) %all-gather.5.cloned.1.call-update) | async-done | bytes 16777232 | tf_op jit(solution)/shard_map/all_gather | solution.py:110
  335.2 11.7 %cholesky.462 = f32[128,128]{1,0:T(8,128)S(1)} custom-call(f32[128,128]{1,0:T(8,128)S(1)} %cholesky.746), custom_call_target="Cholesky" | custom-call | tf_op jit(solution)/shard_map/jit(cholesky)/cholesky | solution.py:21
  347.0 9.8 custom-call.47
  357.6 11.7 %cholesky.481 = f32[128,128]{1,0:T(8,128)S(1)} custom-call(f32[128,128]{1,0:T(8,128)S(1)} %cholesky.750), custom_call_target="Cholesky" | custom-call | tf_op jit(solution)/shard_map/jit(cholesky)/cholesky | solution.py:21
  369.3 10.0 custom-call.48
  380.0 11.7 %cholesky.502 = f32[128,128]{1,0:T(8,128)S(1)} custom-call(f32[128,128]{1,0:T(8,128)S(1)} %cholesky.755), custom_call_target="Cholesky" | custom-call | tf_op jit(solution)/shard_map/jit(cholesky)/cholesky | solution.py:21
  392.4 9.8 custom-call.49
  402.8 12.1 %cholesky.519 = f32[128,128]{1,0:T(8,128)S(1)} custom-call(f32[128,128]{1,0:T(8,128)S(1)} %convolution_subtract_fusion.20), custom_call_target="Cholesky" | custom-call | tf_op jit(solution)/shard_map/jit(cholesky)/cholesky | solution.py:21
  420.1 7.7 while.11
  427.8 39.3 %custom-call.32 = f32[4,128,128]{1,2,0:T(8,128)S(1)} custom-call(f32[4,128,128]{2,1,0:T(8,128)S(1)} %get-tuple-element.21), custom_call_target="InvertDiagBlocksLowerTriangular" | custom-call | tf_op jit(solution)/shard_map/triangular_solve | solution.py:23
  478.0 3.4 convolution_subtract_fusion.1
  482.8 19.3 %slice_subtract_fusion = f32[1536,1536]{0,1:T(8,128)S(1)} fusion(f32[2048,2048]{0,1:T(8,128)} %all-gather.5.cloned.1.call-done, f32[1536,128]{1,0:T(8,128)S(1)} %fusion.200, f32[1536,128]{1,0:T(8,128)S(1)} %copy.46, f32[1536,128]{1,0:T(8,128)S(1)} %copy.45, f32[1536,128]{1,0:T(8,128)S(1)} %copy.44), kind=kOutput, calls=%fused_computation.26 | convolution fusion | flops 14500233216 | bytes 22020096 | tf_op jit(solution)/shard_map/dot_general | solution.py:29
  502.1 3.6 copy-done
  510.8 11.7 %cholesky.534 = f32[128,128]{1,0:T(8,128)S(1)} custom-call(f32[128,128]{1,0:T(8,128)S(1)} %cholesky.759), custom_call_target="Cholesky" | custom-call | tf_op jit(solution)/shard_map/jit(cholesky)/cholesky | solution.py:21
  522.7 9.8 custom-call.50
  535.7 11.7 %cholesky.553 = f32[128,128]{1,0:T(8,128)S(1)} custom-call(f32[128,128]{1,0:T(8,128)S(1)} %cholesky.763), custom_call_target="Cholesky" | custom-call | tf_op jit(solution)/shard_map/jit(cholesky)/cholesky | solution.py:21
  548.7 10.2 custom-call.51
  562.0 13.2 %cholesky.574 = f32[128,128]{1,0:T(8,128)} custom-call(f32[128,128]{1,0:T(8,128)} %cholesky.768), custom_call_target="Cholesky" | custom-call | tf_op jit(solution)/shard_map/jit(cholesky)/cholesky | solution.py:21
  577.3 11.3 %custom-call.52 = f32[1,128,128]{1,2,0:T(8,128)} custom-call(f32[1,128,128]{2,1,0:T(8,128)} %get-tuple-element.139), custom_call_target="InvertDiagBlocksLowerTriangular" | custom-call | tf_op jit(solution)/shard_map/jit(cholesky)/cholesky | solution.py:21
  590.9 11.7 %cholesky.591 = f32[128,128]{1,0:T(8,128)S(1)} custom-call(f32[128,128]{1,0:T(8,128)S(1)} %convolution_subtract_fusion.19), custom_call_target="Cholesky" | custom-call | tf_op jit(solution)/shard_map/jit(cholesky)/cholesky | solution.py:21
  607.5 11.6 %while.12 = (s32[]{:T(128)}, f32[512,512]{1,0:T(8,128)}, s32[4,2]{0,1:T(2,128)S(1)}, f32[4,128,128]{2,1,0:T(8,128)S(1)}, s32[]{:T(128)}) while((s32[]{:T(128)}, f32[512,512]{1,0:T(8,128)}, s32[4,2]{0,1:T(2,128)S(1)}, f32[4,128,128]{2,1,0:T(8,128)S(1)}, s32[]{:T(128)}) %tuple.130), condition=%wide.while_cond.2, body=%wide.while_body.2.sunk | while | flops 2 | bytes 131181 | solution.py:23
  619.0 39.3 %custom-call.33 = f32[4,128,128]{1,2,0:T(8,128)S(1)} custom-call(f32[4,128,128]{2,1,0:T(8,128)S(1)} %get-tuple-element.29), custom_call_target="InvertDiagBlocksLowerTriangular" | custom-call | tf_op jit(solution)/shard_map/triangular_solve | solution.py:23
  676.1 10.0 slice_subtract_fusion.1
  693.1 11.7 %cholesky.606 = f32[128,128]{1,0:T(8,128)S(1)} custom-call(f32[128,128]{1,0:T(8,128)S(1)} %cholesky.772), custom_call_target="Cholesky" | custom-call | tf_op jit(solution)/shard_map/jit(cholesky)/cholesky | solution.py:21
  705.0 9.8 custom-call.53
  718.0 11.7 %cholesky.625 = f32[128,128]{1,0:T(8,128)S(1)} custom-call(f32[128,128]{1,0:T(8,128)S(1)} %cholesky.776), custom_call_target="Cholesky" | custom-call | tf_op jit(solution)/shard_map/jit(cholesky)/cholesky | solution.py:21
  731.1 10.2 custom-call.54
  744.5 13.2 %cholesky.646 = f32[128,128]{1,0:T(8,128)} custom-call(f32[128,128]{1,0:T(8,128)} %cholesky.781), custom_call_target="Cholesky" | custom-call | tf_op jit(solution)/shard_map/jit(cholesky)/cholesky | solution.py:21
  759.8 11.3 %custom-call.55 = f32[1,128,128]{1,2,0:T(8,128)} custom-call(f32[1,128,128]{2,1,0:T(8,128)} %get-tuple-element.129), custom_call_target="InvertDiagBlocksLowerTriangular" | custom-call | tf_op jit(solution)/shard_map/jit(cholesky)/cholesky | solution.py:21
  773.3 11.7 %cholesky.663 = f32[128,128]{1,0:T(8,128)S(1)} custom-call(f32[128,128]{1,0:T(8,128)S(1)} %convolution_subtract_fusion.18), custom_call_target="Cholesky" | custom-call | tf_op jit(solution)/shard_map/jit(cholesky)/cholesky | solution.py:21
  790.0 11.6 %while.13 = (s32[]{:T(128)}, f32[512,512]{1,0:T(8,128)}, s32[4,2]{0,1:T(2,128)S(1)}, f32[4,128,128]{2,1,0:T(8,128)S(1)}, s32[]{:T(128)}) while((s32[]{:T(128)}, f32[512,512]{1,0:T(8,128)}, s32[4,2]{0,1:T(2,128)S(1)}, f32[4,128,128]{2,1,0:T(8,128)S(1)}, s32[]{:T(128)}) %tuple.131), condition=%wide.while_cond.3, body=%wide.while_body.3.sunk | while | flops 2 | bytes 131181 | solution.py:23
  801.6 39.3 %custom-call.34 = f32[4,128,128]{1,2,0:T(8,128)S(1)} custom-call(f32[4,128,128]{2,1,0:T(8,128)S(1)} %get-tuple-element.37), custom_call_target="InvertDiagBlocksLowerTriangular" | custom-call | tf_op jit(solution)/shard_map/triangular_solve | solution.py:23
  853.4 3.6 convolution_subtract_fusion.3
  862.2 11.7 %cholesky.678 = f32[128,128]{1,0:T(8,128)S(1)} custom-call(f32[128,128]{1,0:T(8,128)S(1)} %cholesky.785), custom_call_target="Cholesky" | custom-call | tf_op jit(solution)/shard_map/jit(cholesky)/cholesky | solution.py:21
  874.5 9.8 custom-call.56
  910.2 11.7 %cholesky.697 = f32[128,128]{1,0:T(8,128)S(1)} custom-call(f32[128,128]{1,0:T(8,128)S(1)} %cholesky.789), custom_call_target="Cholesky" | custom-call | tf_op jit(solution)/shard_map/jit(cholesky)/cholesky | solution.py:21
  924.6 9.8 custom-call.57
  937.7 11.9 %cholesky.718 = f32[128,128]{1,0:T(8,128)S(1)} custom-call(f32[128,128]{1,0:T(8,128)S(1)} %cholesky.794), custom_call_target="Cholesky" | custom-call | tf_op jit(solution)/shard_map/jit(cholesky)/cholesky | solution.py:21
  950.8 9.8 custom-call.58
  962.9 11.7 %cholesky.735 = f32[128,128]{1,0:T(8,128)S(1)} custom-call(f32[128,128]{1,0:T(8,128)S(1)} %convolution_subtract_fusion.17), custom_call_target="Cholesky" | custom-call | tf_op jit(solution)/shard_map/jit(cholesky)/cholesky | solution.py:21
  982.1 14.3 %while.14 = (s32[]{:T(128)}, f32[512,512]{1,0:T(8,128)}, s32[4,2]{0,1:T(2,128)S(1)}, f32[4,128,128]{2,1,0:T(8,128)}, s32[]{:T(128)}) while((s32[]{:T(128)}, f32[512,512]{1,0:T(8,128)}, s32[4,2]{0,1:T(2,128)S(1)}, f32[4,128,128]{2,1,0:T(8,128)}, s32[]{:T(128)}) %tuple.132), condition=%wide.while_cond.clone.2, body=%wide.while_body.clone.2.sunk | while | flops 2 | bytes 132705 | solution.py:57
  996.3 40.9 %custom-call.62 = f32[4,128,128]{1,2,0:T(8,128)} custom-call(f32[4,128,128]{2,1,0:T(8,128)} %get-tuple-element.59), custom_call_target="InvertDiagBlocksLowerTriangular" | custom-call | tf_op jit(solution)/shard_map/triangular_solve/custom-call.10 | solution.py:57
  1037.6 6.1 fusion.59
  (336 shorter events, 201.4 us)
Async XLA Ops:
  7.2 141.2 %all-reduce.4.cloned.1.call-start = ((), (), s32[]{:S(2)}) async-start(), calls=%async_computation.1 | async-start | bytes 2097152 | tf_op jit(solution)/shard_map/psum | solution.py:9
  30.8 20.2 %copy-start.6 = (bf16[2,1,2048,64]{2,3,0,1:T(8,128)(2,1)}, bf16[2,1,2048,64]{2,3,0,1:T(8,128)(2,1)S(1)}, u32[]{:S(2)}) copy-start(bf16[2,1,2048,64]{2,3,0,1:T(8,128)(2,1)S(1)} %all_gather.12) | copy-start | bytes 1572868
  54.2 96.1 %copy-start.50 = (bf16[2,1,4,2048]{3,2,1,0:T(4,128)(2,1)S(1)}, bf16[2,1,4,2048]{3,2,1,0:T(4,128)(2,1)}, u32[]{:S(2)}) copy-start(bf16[2,1,4,2048]{3,2,1,0:T(4,128)(2,1)} %param.13) | copy-start | bytes 98308
  54.2 96.1 %copy-start.54 = (s32[2,1]{0,1:T(1,128)S(1)}, s32[2,1]{0,1:T(1,128)}, u32[]{:S(2)}) copy-start(s32[2,1]{0,1:T(1,128)} %param.14) | copy-start | bytes 28
  54.3 173.1 %copy-start.7 = (bf16[2,1,2048,64]{2,3,0,1:T(8,128)(2,1)S(1)}, bf16[2,1,2048,64]{2,3,0,1:T(8,128)(2,1)}, u32[]{:S(2)}) copy-start(bf16[2,1,2048,64]{2,3,0,1:T(8,128)(2,1)} %copy-done.6) | copy-start | bytes 1572868
  54.3 173.0 %all-gather.3.cloned.1.call-start = ((), (), s32[]{:S(2)}) async-start(), calls=%async_computation | async-start | bytes 8912896 | tf_op jit(solution)/shard_map/all_gather | solution.py:86
  55.0 277.1 %all-gather.5.cloned.1.call-start = ((), (), s32[]{:S(2)}) async-start(), calls=%async_computation.2 | async-start | bytes 17825792 | tf_op jit(solution)/shard_map/all_gather | solution.py:110
  427.8 41.7 %copy-start.16 = (f32[512,512]{1,0:T(8,128)}, f32[512,512]{1,0:T(8,128)S(1)}, u32[]{:S(2)}) copy-start(f32[512,512]{1,0:T(8,128)S(1)} %get-tuple-element.348) | copy-start | bytes 3145732
  467.1 14.2 %copy-start.25 = (f32[4,128,128]{1,2,0:T(8,128)}, f32[4,128,128]{1,2,0:T(8,128)S(1)}, u32[]{:S(2)}) copy-start(f32[4,128,128]{1,2,0:T(8,128)S(1)} %custom-call.32) | copy-start | bytes 786436
  472.4 2.5 copy-start.4
  482.8 19.3 %copy-start.2 = (f32[1536,128]{1,0:T(8,128)}, f32[1536,128]{1,0:T(8,128)S(1)}, u32[]{:S(2)}) copy-start(f32[1536,128]{1,0:T(8,128)S(1)} %fusion.200) | copy-start | bytes 2359300
  502.1 3.6 copy-start
  673.8 12.3 %copy-start.11 = (f32[1024,128]{1,0:T(8,128)}, f32[1024,128]{1,0:T(8,128)S(1)}, u32[]{:S(2)}) copy-start(f32[1024,128]{1,0:T(8,128)S(1)} %copy.50) | copy-start | bytes 1572868
  676.1 10.0 copy-start.13
  840.9 10.1 copy-start.28
  859.3 36.1 %copy-start.3 = (f32[1536,128]{1,0:T(8,128)S(1)}, f32[1536,128]{1,0:T(8,128)}, u32[]{:S(2)}) copy-start(f32[1536,128]{1,0:T(8,128)} %copy-done.2) | copy-start | bytes 2359300
  886.2 10.9 %copy-start.27 = (f32[4,128,128]{1,2,0:T(8,128)S(1)}, f32[4,128,128]{1,2,0:T(8,128)}, u32[]{:S(2)}) copy-start(f32[4,128,128]{1,2,0:T(8,128)} %copy-done.26) | copy-start | bytes 786436
  886.2 15.2 %copy-start.9 = (f32[1024,128]{1,0:T(8,128)S(1)}, f32[1024,128]{1,0:T(8,128)}, u32[]{:S(2)}) copy-start(f32[1024,128]{1,0:T(8,128)} %copy.52) | copy-start | bytes 1572868
  886.2 15.2 %copy-start.10 = (f32[1024,128]{1,0:T(8,128)S(1)}, f32[1024,128]{1,0:T(8,128)}, u32[]{:S(2)}) copy-start(f32[1024,128]{1,0:T(8,128)} %copy.51) | copy-start | bytes 1572868
  886.2 15.2 %copy-start.12 = (f32[1024,128]{1,0:T(8,128)S(1)}, f32[1024,128]{1,0:T(8,128)}, u32[]{:S(2)}) copy-start(f32[1024,128]{1,0:T(8,128)} %copy-done.11) | copy-start | bytes 1572868
  886.2 15.2 %copy-start.14 = (f32[1024,128]{1,0:T(8,128)S(1)}, f32[1024,128]{1,0:T(8,128)}, u32[]{:S(2)}) copy-start(f32[1024,128]{1,0:T(8,128)} %copy-done.13) | copy-start | bytes 1572868
  886.2 15.2 %copy-start.17 = (f32[512,512]{1,0:T(8,128)S(1)}, f32[512,512]{1,0:T(8,128)}, u32[]{:S(2)}) copy-start(f32[512,512]{1,0:T(8,128)} %get-tuple-element.107) | copy-start | bytes 3145732
  886.2 15.2 %copy-start.18 = (f32[512,512]{1,0:T(8,128)S(1)}, f32[512,512]{1,0:T(8,128)}, u32[]{:S(2)}) copy-start(f32[512,512]{1,0:T(8,128)} %get-tuple-element.105) | copy-start | bytes 3145732
  887.8 22.4 %copy-start.30 = (f32[384,128]{1,0:T(8,128)}, f32[384,128]{1,0:T(8,128)S(1)}, u32[]{:S(2)}) copy-start(f32[384,128]{1,0:T(8,128)S(1)} %convolution_subtract_fusion.9) | copy-start | bytes 589828
  893.1 8.3 copy-start.38
  895.4 8.9 copy-start.44
  898.5 5.8 copy-start.40
  899.8 4.5 copy-start.46
  901.2 3.1 copy-start.51
  901.5 2.9 copy-start.19
  901.5 2.9 copy-start.29
  901.5 7.6 copy-start.34
  901.5 22.4 %copy-start.55 = (f32[128]{0:T(128)S(1)}, f32[128]{0:T(128)}, u32[]{:S(2)}) copy-start(f32[128]{0:T(128)} %get-tuple-element.124) | copy-start | bytes 1540
  904.5 29.9 %copy-start.36 = (f32[128,8]{0,1:T(8,128)}, f32[128,8]{0,1:T(8,128)S(1)}, u32[]{:S(2)}) copy-start(f32[128,8]{0,1:T(8,128)S(1)} %fusion.208) | copy-start | bytes 12292
  905.7 4.5 copy-start.42
  907.0 3.2 copy-start.48
  978.4 59.1 %copy-start.23 = (f32[512,128]{1,0:T(8,128)S(1)}, f32[512,128]{1,0:T(8,128)}, u32[]{:S(2)}) copy-start(f32[512,128]{1,0:T(8,128)} %copy.58) | copy-start | bytes 786436
  978.4 59.1 %copy-start.37 = (f32[128,8]{0,1:T(8,128)S(1)}, f32[128,8]{0,1:T(8,128)}, u32[]{:S(2)}) copy-start(f32[128,8]{0,1:T(8,128)} %copy-done.36) | copy-start | bytes 12292
  978.4 59.1 %copy-start.39 = (f32[128,8]{0,1:T(8,128)S(1)}, f32[128,8]{0,1:T(8,128)}, u32[]{:S(2)}) copy-start(f32[128,8]{0,1:T(8,128)} %copy-done.38) | copy-start | bytes 12292
  978.4 59.1 %copy-start.41 = (f32[128,8]{0,1:T(8,128)S(1)}, f32[128,8]{0,1:T(8,128)}, u32[]{:S(2)}) copy-start(f32[128,8]{0,1:T(8,128)} %copy-done.40) | copy-start | bytes 12292
  978.4 59.1 %copy-start.43 = (f32[128,8]{0,1:T(8,128)S(1)}, f32[128,8]{0,1:T(8,128)}, u32[]{:S(2)}) copy-start(f32[128,8]{0,1:T(8,128)} %copy-done.42) | copy-start | bytes 12292
  978.4 59.1 %copy-start.45 = (f32[128,8]{0,1:T(8,128)S(1)}, f32[128,8]{0,1:T(8,128)}, u32[]{:S(2)}) copy-start(f32[128,8]{0,1:T(8,128)} %copy-done.44) | copy-start | bytes 12292
  978.4 59.1 %copy-start.47 = (f32[128,8]{0,1:T(8,128)S(1)}, f32[128,8]{0,1:T(8,128)}, u32[]{:S(2)}) copy-start(f32[128,8]{0,1:T(8,128)} %copy-done.46) | copy-start | bytes 12292
  978.4 59.1 %copy-start.49 = (f32[128,8]{0,1:T(8,128)S(1)}, f32[128,8]{0,1:T(8,128)}, u32[]{:S(2)}) copy-start(f32[128,8]{0,1:T(8,128)} %copy-done.48) | copy-start | bytes 12292
  978.5 59.1 %copy-start.52 = (f32[128,8]{0,1:T(8,128)S(1)}, f32[128,8]{0,1:T(8,128)}, u32[]{:S(2)}) copy-start(f32[128,8]{0,1:T(8,128)} %copy-done.51) | copy-start | bytes 12292
  978.5 59.1 %copy-start.53 = (f32[128,8]{0,1:T(8,128)S(1)}, f32[128,8]{0,1:T(8,128)}, u32[]{:S(2)}) copy-start(f32[128,8]{0,1:T(8,128)} %fusion.213) | copy-start | bytes 12292
  1037.6 6.1 copy-start.8
  1037.6 6.1 copy-start.35
  (11 other events, 11.1 us)
Sparse Core Ops, SparseCore 0:
  54.4 93.9 all-reduce.3
  150.8 76.4 all-gather.2
  229.1 103.0 all-gather.4
where the time goes:
time: 1060 us
  other arithmetic  505 us (48%)
  waiting for transfers between devices  272 us (26%)
  matrix products  132 us (12%)
  local copies, waits for them, and re-layouts  84.2 us (8%)
  blocking collectives  38.6 us (4%)
  between operations  25.3 us (2%)
    another operation x59, other arithmetic, blocked_cholesky(): diagonal_factor = jnp.linalg.cholesky(diagonal_block)  328 us
    another operation x7, other arithmetic, blocked_cholesky(): lax.linalg.triangular_solve(diagonal_factor, lower_block, left_side=False...  122 us
    all_gather x1, waiting for transfers between devices, body(): lead_tile = lax.all_gather(lead_rows, 'col', axis=0, tiled=True)  102 us
    psum x1, waiting for transfers between devices, spread(): return lax.psum(kept, axis)  93.3 us
    all_gather x1, waiting for transfers between devices, body(): all_tiles = lax.all_gather(right_full, 'row', axis=1, tiled=True)  76.1 us
    another operation x2, other arithmetic, blocked_forward(): lax.linalg.triangular_solve(diagonal_factor, target, left_side=True, lowe...  43.8 us
    another operation x21, matrix products, blocked_cholesky(): lax.linalg.triangular_solve(diagonal_factor, lower_block, left_side=False...  36.3 us
    dot_general x3, matrix products, blocked_cholesky(): jnp.dot(lower_factor, lower_factor.T, precision=lax.Precision.HIGHEST, pr...  33 us
  transfers between devices with their start and end apart: 3, of which 3 were waited for; matrix products, arithmetic and copies ran while one was open for 1% of the time, Pallas kernels for 0%

commit v1 on v0

v1 whole, which is shorter than its diff:
```python
import jax, jax.numpy as jnp
from jax import lax
from jax.sharding import PartitionSpec as P
from jax.experimental import pallas as pl
from jax.experimental.pallas import tpu as pltpu

BLK = 128
GRP = 8

def recip(value):
    start = pl.reciprocal(value, approx=True)
    return start * (2.0 - value * start)

def invert_factor(rows):
    count = len(rows)
    lanes = lax.broadcasted_iota(jnp.int32, (GRP, BLK), 1)
    subs = lax.broadcasted_iota(jnp.int32, (GRP, BLK), 0)
    shape = (GRP, BLK)
    rows = list(rows)
    out = []
    for g in range(count):
        base = g * GRP
        here = (lanes >= base) & (lanes < base + GRP)
        cols = {
            h: [jnp.broadcast_to(rows[h][:, base + j : base + j + 1], shape) for j in range(GRP)]
            for h in range(g, count)
        }
        tri = {
            (i, j): jnp.broadcast_to(cols[g][j][i : i + 1, :], shape)
            for j in range(GRP)
            for i in range(j, GRP)
        }
        pivot = jnp.where(here, jnp.where(lanes - base == subs, 1.0, 0.0), rows[g])
        lines = [jnp.broadcast_to(pivot[j : j + 1, :], shape) for j in range(GRP)]
        inv = []
        unit = {}
        for j in range(GRP):
            inv.append(recip(tri[j, j]))
            for i in range(j + 1, GRP):
                unit[i, j] = tri[i, j] * inv[j]
            for i in range(j + 1, GRP):
                for k in range(j + 1, i + 1):
                    tri[i, k] = tri[i, k] - unit[i, j] * tri[k, j]
                lines[i] = lines[i] - unit[i, j] * lines[j]
        done = lines[0] * lax.rsqrt(tri[0, 0])
        for j in range(1, GRP):
            done = jnp.where(subs == j, lines[j] * lax.rsqrt(tri[j, j]), done)
        out.append(jnp.where(lanes <= subs + base, done, 0.0))
        if g + 1 < count:
            back = [None] * GRP
            for j in range(GRP - 1, -1, -1):
                acc = lines[j] * inv[j]
                for i in range(GRP - 1, j, -1):
                    acc = acc - unit[i, j] * back[i]
                back[j] = acc
            for h in range(g + 1, count):
                acc = jnp.where(here, 0.0, rows[h])
                for j in range(GRP - 1, -1, -1):
                    acc = acc - cols[h][j] * back[j]
                rows[h] = acc
    return out

NT = (((1,), (1,)), ((), ()))

def halves(value):
    high = value.astype(jnp.bfloat16)
    return high, (value - high.astype(jnp.float32)).astype(jnp.bfloat16)

def mul3(lh, ll, rh, rl):
    def one(x, y):
        return lax.dot_general(x, y, NT, preferred_element_type=jnp.float32)
    return one(lh, rh) + (one(lh, rl) + one(ll, rh))

def chol_kernel(pos_ref, lead_ref, y_ref, x_ref, part_ref, high, low, work, wh, wl):
    order = y_ref.shape[1]
    count = order // BLK
    extra = y_ref.shape[0]
    total = order + extra
    row, col = pos_ref[0], pos_ref[1]

    def block_of(i, k):
        apart = i - k
        source, slot = (i, apart) if 2 * apart <= count else (k, count - apart)
        return lead_ref[source % 2, source // 2, slot]

    def given(r0, r1, k):
        lo = k * BLK
        parts = [block_of(r // BLK, k) for r in range(r0, min(r1, order), BLK)]
        if r1 > order:
            parts.append(y_ref[max(r0, order) - order:r1 - order, lo:lo + BLK])
        return parts[0] if len(parts) == 1 else jnp.concatenate(parts, axis=0)

    for r in range(0, order, BLK):
        work[r:r + BLK, :] = block_of(r // BLK, 0)
    work[order:, :] = y_ref[:, :BLK]
    part_ref[...] = jnp.zeros_like(part_ref)

    def spans(start):
        return [(r, min(r + 2 * BLK, total)) for r in range(start, total, 2 * BLK)]

    def step(k, carry):
        base = pl.multiple_of(k * BLK, BLK)
        rows = [work[pl.ds(base + g * GRP, GRP), :] for g in range(BLK // GRP)]
        inverse = invert_factor(rows)
        full = jnp.concatenate(inverse, axis=0)
        high_part, low_part = halves(full)
        wh[...] = high_part
        wl[...] = low_part

        for s in range(count):
            @pl.when(k == s)
            def _(s=s):
                lo, hi = s * BLK, s * BLK + BLK
                for r0, r1 in spans(lo):
                    sh, sl = halves(work[r0:r1, :])
                    panel = mul3(sh, sl, wh[...], wl[...])
                    ph, pl_ = halves(panel)
                    high[r0:r1, lo:hi] = ph
                    low[r0:r1, lo:hi] = pl_
                    work[r0:r1, :] = panel
                x_ref[:, lo:hi] = work[order:order + x_ref.shape[0], :]

                @pl.when(jnp.logical_and(col == s, row >= s))
                def _():
                    block = work[pl.ds(pl.multiple_of(row * BLK, BLK), BLK), :]
                    r = lax.broadcasted_iota(jnp.int32, (BLK, BLK), 0)
                    c = lax.broadcasted_iota(jnp.int32, (BLK, BLK), 1)
                    part_ref[...] = jnp.where((row > s) | (r >= c), block, 0.0)

                if s + 1 < count:
                    for r0, r1 in spans(hi):
                        work[r0:r1, :] = given(r0, r1, s + 1) - mul3(
                            high[r0:r1, :hi], low[r0:r1, :hi],
                            high[hi:hi + BLK, :hi], low[hi:hi + BLK, :hi])
        return carry

    lax.fori_loop(0, count, step, 0)

def chol_call(pos, lead, right, count):
    extra, order = right.shape
    vm = pl.BlockSpec(memory_space=pltpu.VMEM)
    return pl.pallas_call(
        chol_kernel,
        out_shape=(jax.ShapeDtypeStruct((count, order), jnp.float32), jax.ShapeDtypeStruct((BLK, BLK), jnp.float32)),
        in_specs=[pl.BlockSpec(memory_space=pltpu.SMEM), vm, vm],
        out_specs=(vm, vm),
        scratch_shapes=[
            pltpu.VMEM((order + extra, order), jnp.bfloat16),
            pltpu.VMEM((order + extra, order), jnp.bfloat16),
            pltpu.VMEM((order + extra, BLK), jnp.float32),
            pltpu.VMEM((BLK, BLK), jnp.bfloat16),
            pltpu.VMEM((BLK, BLK), jnp.bfloat16),
        ],
        compiler_params=pltpu.CompilerParams(vmem_limit_bytes=58 * 2**20),
        cost_estimate=pl.CostEstimate(flops=10**11, bytes_accessed=2 * 10**8, transcendentals=0),
    )(pos, lead, right)


def exchange_kernel(
    vu_ref, diag_ref, vu_all, vv_all, lead,
    blocks, piece, pairs, um,
    uv_send, uv_recv, fw_send, fw_recv, cut_send, cut_recv, ring_send, ring_recv,
    flat_send, flat_recv, pair_send, pair_recv, vcut_send, vcut_recv, vflat_send, vflat_recv, local_sem,
):
    rows, cols = flat_send.shape[0], vu_all.shape[0]
    depth = cols // 2
    thin = piece.shape[2]
    band = lead.shape[2]
    p, c = lax.axis_index("row"), lax.axis_index("col")
    z, core = c // 2, lax.rem(c, 2)
    sibling = c + 1 - 2 * core

    def along(d):
        return (p, 2 * lax.rem(z + d, depth) + core)

    def plane(d):
        return (lax.rem(p + d, rows), c)

    def remote(src, dst, send, recv, where):
        return pltpu.make_async_remote_copy(
            src_ref=src, dst_ref=dst, send_sem=send, recv_sem=recv,
            device_id=where, device_id_type=pl.DeviceIdType.MESH,
        )

    barrier = pltpu.get_barrier_semaphore()
    partners = [along(d) for d in range(1, depth)] + [(p, sibling)] + [plane(d) for d in range(1, rows)]
    for where in partners:
        pl.semaphore_signal(barrier, inc=1, device_id=where, device_id_type=pl.DeviceIdType.MESH)
    pl.semaphore_wait(barrier, len(partners))

    pending = []

    def spread_start(a):
        first = []
        for d in range(1, depth):
            copy = remote(vu_ref.at[a], vu_all.at[c, a], uv_send.at[a, d], uv_recv.at[a, d], along(d))
            copy.start()
            first.append(copy)
        own = remote(vu_ref.at[a], vu_all.at[c, a], fw_send.at[a, 0], fw_recv.at[a, 0], (p, sibling))
        own.start()
        vu_all[c, a] = vu_ref[a]
        return first, own

    def spread_end(a, first, own):
        later = [own]
        for d in range(1, depth):
            first[d - 1].wait_recv()
            held = vu_all.at[2 * lax.rem(z + depth - d, depth) + core, a]
            copy = remote(held, held, fw_send.at[a, d], fw_recv.at[a, d], (p, sibling))
            copy.start()
            later.append(copy)
        for copy in later:
            copy.wait_recv()
        pending.extend(first + later)

    first, own = spread_start(0)
    spread_end(0, first, own)

    cuts = [
        remote(blocks.at[:, pl.ds(d * thin, thin), :], piece.at[z], cut_send.at[d], cut_recv, (d, c))
        for d in range(1, rows)
    ]

    @pl.when(p == 0)
    def _():
        size = BLK
        r = lax.broadcasted_iota(jnp.int32, (size, size), 0)
        l = lax.broadcasted_iota(jnp.int32, (size, size), 1)
        half = size // 2

        def dots(x, y, dims):
            return lax.dot_general(x, y, (dims, ((), ())), preferred_element_type=jnp.float32)

        gram = jnp.zeros((size, size), jnp.float32)
        for s in range(cols):
            slab = vu_all[s, 0]
            gram = gram + dots(slab, slab, ((0,), (0,)))
        core_w = jnp.where((r < half) & (l < half), gram, 0.0).astype(jnp.bfloat16)
        down = jnp.where(r == l + half, 1.0, 0.0).astype(jnp.bfloat16)
        right = jnp.where(l == r + half, 1.0, 0.0).astype(jnp.bfloat16)
        same = jnp.where((r == l) & (r >= half), 1.0, 0.0)
        low_w = dots(down, core_w, ((1,), (0,)))
        low_w16 = low_w.astype(jnp.bfloat16)
        take_mu = (low_w + same).astype(jnp.bfloat16)
        take_um = (dots(low_w16, right, ((1,), (0,))) + down.astype(jnp.float32)).astype(jnp.bfloat16)
        for s in range(cols):
            um[s] = dots(vu_all[s, 0], take_um, ((1,), (0,))).astype(jnp.bfloat16)
        mine = dots(vu_ref[0], take_mu, ((1,), (0,))).astype(jnp.bfloat16)
        for j in range(band):
            other = lax.rem(c + cols - j, cols)
            fix = dots(mine, um[other], ((1,), (1,)))
            block = diag_ref[:, pl.ds(pl.multiple_of(other * size, size), size)] - 0.5 * fix

            @pl.when(c >= j)
            def _(block=block, j=j):
                blocks[j] = block

            @pl.when(c < j)
            def _(block=block, j=j):
                blocks[j] = block.T
        piece[z] = blocks[:, :thin, :]
        for copy in cuts:
            copy.start()

    @pl.when(p > 0)
    def _():
        cuts[0].wait_recv()

    ring = []
    for d in range(1, depth):
        copy = remote(piece.at[z], piece.at[z], ring_send.at[d], ring_recv.at[d], along(d))
        copy.start()
        ring.append(copy)
    first, own = spread_start(1)
    for copy in ring:
        copy.wait_recv()

    def place(q):
        return lead.at[core, :, :, pl.ds(pl.multiple_of(q * thin, thin), thin), :]

    flats = []
    for d in range(1, rows):
        copy = remote(piece, place(p), flat_send.at[d], flat_recv.at[d], plane(d))
        copy.start()
        flats.append(copy)
    keep = pltpu.make_async_copy(piece, place(p), local_sem)
    keep.start()
    halfway = [remote(piece, place(p), pair_send.at[0], pair_recv.at[0], (p, sibling))]
    halfway[0].start()

    spread_end(1, first, own)
    vcuts = [remote(pairs.at[d], vv_all.at[lax.rem(p + d, rows)], vcut_send.at[d], vcut_recv, plane(d)) for d in range(1, rows)]

    @pl.when(p == c)
    def _():
        for s in range(cols):
            d = lax.rem(s + rows - p, rows)
            lanes = lax.broadcasted_iota(jnp.int32, (BLK, BLK), 1)
            lefts = vu_all[s, 0].astype(jnp.float32)
            rights = pltpu.roll(vu_all[s, 1].astype(jnp.float32), BLK // 2, 1)
            pairs[d] = jnp.where(lanes < BLK // 2, lefts, rights).astype(jnp.bfloat16)
        vv_all[p] = pairs[0]
        for copy in vcuts:
            copy.start()

    @pl.when(p != c)
    def _():
        vcuts[0].wait_recv()

    vflats = []
    for d in range(1, rows):
        copy = remote(vv_all.at[p], vv_all.at[p], vflat_send.at[d], vflat_recv.at[d], plane(d))
        copy.start()
        vflats.append(copy)

    for d in range(1, rows):
        flats[d - 1].wait_recv()
        held = place(lax.rem(p + rows - d, rows))
        copy = remote(held, held, pair_send.at[d], pair_recv.at[d], (p, sibling))
        copy.start()
        halfway.append(copy)
    keep.wait()
    for copy in halfway + vflats:
        copy.wait_recv()
    for copy in pending + ring + flats + halfway + vflats:
        copy.wait_send()

    @pl.when(p == 0)
    def _():
        for copy in cuts:
            copy.wait_send()

    @pl.when(p == c)
    def _():
        for copy in vcuts:
            copy.wait_send()


def exchange(vu, diag_rows):
    rows, cols = lax.axis_size("row"), lax.axis_size("col")
    depth, band, thin = cols // 2, cols // 2 + 1, BLK // rows
    vm = pl.BlockSpec(memory_space=pltpu.VMEM)
    dma = pltpu.SemaphoreType.DMA
    return pl.pallas_call(
        exchange_kernel,
        out_shape=(
            jax.ShapeDtypeStruct((cols, 2, BLK, BLK), jnp.bfloat16),
            jax.ShapeDtypeStruct((cols, BLK, BLK), jnp.bfloat16),
            jax.ShapeDtypeStruct((2, depth, band, BLK, BLK), jnp.float32),
        ),
        in_specs=[vm, vm],
        out_specs=(vm, vm, pl.BlockSpec(memory_space=pl.ANY)),
        scratch_shapes=[
            pltpu.VMEM((band, BLK, BLK), jnp.float32),
            pltpu.VMEM((depth, band, thin, BLK), jnp.float32),
            pltpu.VMEM((cols, BLK, BLK), jnp.bfloat16),
            pltpu.VMEM((cols, BLK, BLK), jnp.bfloat16),
            dma((2, depth)), dma((2, depth)), dma((2, depth)), dma((2, depth)),
            dma((rows,)), dma, dma((depth,)), dma((depth,)),
            dma((rows,)), dma((rows,)), dma((rows,)), dma((rows,)),
            dma((rows,)), dma, dma((rows,)), dma((rows,)), dma,
        ],
        compiler_params=pltpu.CompilerParams(
            collective_id=0, has_side_effects=True, vmem_limit_bytes=40 * 2**20
        ),
    )(vu, diag_rows)


def body(pan_left, pan_right, panel_rank, diag_tiles, col_right, column_rank):
    tile_rows = pan_left.shape[0]
    slab_rows = pan_left.shape[2]
    rank_width = pan_left.shape[3]
    tile_order = diag_tiles.shape[3]
    row_count = lax.axis_size("row")
    col_count = lax.axis_size("col")
    row_index = lax.axis_index("row")
    col_index = lax.axis_index("col")
    col_tiles = tile_rows * row_count // col_count
    columns = lax.broadcasted_iota(jnp.int32, pan_left.shape, 3)
    keep_mask = columns < panel_rank[:, :, None, None]
    zeros_half = jnp.zeros_like(pan_left)
    left_masked = jnp.where(keep_mask, pan_left, zeros_half)
    right_masked = jnp.where(keep_mask, pan_right, zeros_half)
    vu = jnp.concatenate([right_masked, left_masked], axis=3)[:, 0]
    vu_all, vv_all, lead = exchange(vu, diag_tiles[0, 0])
    flat_vu = vu_all.transpose(1, 0, 2, 3).reshape(tile_rows, tile_order, 2 * rank_width)
    right_tiles, left_tiles = flat_vu[:, :, :rank_width], flat_vu[:, :, rank_width:]
    theirs = vv_all.reshape(tile_order, col_tiles, rank_width)
    own_gram = jnp.einsum(
        "anr,ans->ars", right_tiles, right_tiles, preferred_element_type=jnp.float32
    ).astype(jnp.bfloat16)
    products = jnp.einsum(
        "anr,ars->ans", left_tiles, own_gram, preferred_element_type=jnp.float32
    ).astype(jnp.bfloat16)
    product_rows = lax.dynamic_slice_in_dim(products, col_index * slab_rows, slab_rows, 1)
    correction = jnp.einsum(
        "ans,ams->anm", product_rows, left_tiles, preferred_element_type=jnp.float32
    )
    diag_new = diag_tiles - correction[:, None]
    cross_gram = jnp.einsum(
        "anr,nbs->abrs", right_tiles, theirs, preferred_element_type=jnp.float32
    ).astype(jnp.bfloat16)

    narrow_rows = col_right.shape[2]
    rank_ids = lax.broadcasted_iota(jnp.int32, col_right.shape, 2) + col_index * narrow_rows
    tile_ids = lax.broadcasted_iota(jnp.int32, col_right.shape, 0) * row_count + row_index
    keep_right = (rank_ids < column_rank[:, :, None, None]) & (tile_ids >= 1)
    right_kept = jnp.where(keep_right, col_right, jnp.zeros_like(col_right))
    right_side = right_kept.astype(jnp.float32).reshape(-1, tile_order)
    count = right_side.shape[0]
    right_side = jnp.pad(right_side, ((0, -count % 16), (0, 0)))
    place = jnp.stack([row_index, col_index]).astype(jnp.int32)
    solved, lead_part = chol_call(place, lead, right_side, count)
    col_solved = solved.reshape(col_right.shape)

    tile_update = jnp.einsum(
        "anr,abrs->abns", left_tiles, cross_gram, preferred_element_type=jnp.float32
    )
    row_ids = lax.broadcasted_iota(jnp.int32, (tile_rows, col_tiles), 0) * row_count + row_index
    col_ids = lax.broadcasted_iota(jnp.int32, (tile_rows, col_tiles), 1) * col_count + col_index
    lower_mask = (row_ids > col_ids)[:, :, None, None]
    panel_update = jnp.where(lower_mask, tile_update, jnp.zeros_like(tile_update)).astype(
        jnp.bfloat16
    )
    panel_update = panel_update.reshape(tile_rows, 1, col_tiles, 1, tile_order, rank_width)
    return (panel_update, diag_new, lead_part, col_solved)


def solution(mesh):
    placed = (
        P(None, "row", "col", None),
        P(None, "row", "col", None),
        P(None, "row"),
        P(None, "row", "col", None),
        P(None, "row", "col", None),
        P(None, "row"),
    )
    return jax.shard_map(
        body,
        mesh=mesh,
        in_specs=placed,
        out_specs=(
            P(None, "row", None, "col", None, None),
            P(None, "row", "col", None),
            P("row", "col"),
            P(None, "row", "col", None),
        ),
        check_vma=False,
    )
```

time: 1060 us -> 285 us (0.27)
  the two profiles are of different devices: /device:TPU:1 before, /device:TPU:192 now
where the time goes in v1:
time: 285 us; the launch traced here: 284 us
  Pallas kernels  266 us (93%)
  local copies, waits for them, and re-layouts  8.17 us (3%)
  matrix products  6.41 us (2%)
  other arithmetic  3.03 us (1%)
    pallas_call x1, Pallas kernels, exchange(): pl.pallas_call(exchange_kernel, out_shape=(jax.ShapeDtypeStruct((cols, 2,...  143 us
    pallas_call x1, Pallas kernels, chol_call(): pl.pallas_call(chol_kernel, out_shape=(jax.ShapeDtypeStruct((count, order...  123 us

profile of v1, /device:TPU:192, one launch (start us, length us, event | category | flops | bytes accessed | tf_op | source)
XLA Modules:
  0.0 284.3 jit_solution(2323926386009506282)
XLA Ops:
  0.6 0.6 pad_add_fusion.pos_ref
  1.2 0.1 broadcast_compare_fusion
  1.3 0.8 and_select_fusion
  2.2 0.9 copy.17
  3.1 0.9 copy.16
  3.9 0.8 fusion.17
  4.7 0.1 maximum_bitcast_fusion.vu_ref
  4.8 0.7 pad_convert_fusion.y_ref
  5.5 1.3 slice_bitcast_fusion.diag_ref
  6.8 142.6 %shard_map.93 = (bf16[16,2,128,128]{3,2,1,0:T(8,128)(2,1)S(1)}, bf16[16,128,128]{2,1,0:T(8,128)(2,1)S(1)}, f32[2,8,9,128,128]{4,3,2,1,0:T(8,128)S(1)}) custom-call(bf16[2,128,128]{2,1,0:T(8,128)(2,1)S(1)} %maximum_bitcast_fusion.vu_ref, f32[128,2048]{1,0:T(8,128)S(1)} %slice_bitcast_fusion.diag_ref), custom_call_target="tpu_custom_call" | custom-call | tf_op jit(solution)/shard_map/pallas_call | solution.py:344
  149.4 0.0 copy-start
  149.4 3.6 %copy-done = f32[2,8,9,128,128]{4,3,2,1,0:T(8,128)} copy-done((f32[2,8,9,128,128]{4,3,2,1,0:T(8,128)}, f32[2,8,9,128,128]{4,3,2,1,0:T(8,128)S(1)}, u32[]{:S(2)}) %copy-start) | copy-done | bytes 9437208
  153.0 123.4 %shard_map.94 = (f32[8,2048]{1,0:T(8,128)}, f32[128,128]{1,0:T(8,128)}) custom-call(s32[2]{0:T(128)} %pad_add_fusion.pos_ref, f32[2,8,9,128,128]{4,3,2,1,0:T(8,128)} %copy-done, f32[16,2048]{1,0:T(8,128)} %pad_convert_fusion.y_ref), custom_call_target="tpu_custom_call" | custom-call | flops 99999997952 | bytes 200000000 | tf_op jit(solution)/shard_map/pallas_call | solution.py:142
  276.4 0.0 copy-start.2
  276.4 0.4 copy.18
  276.8 0.2 reshape.76
  277.1 0.1 copy.19
  277.2 0.1 copy-done.2
  277.2 0.7 reshape.75
  277.9 1.9 fusion.3
  279.8 0.0 copy-start.1
  279.8 1.7 fusion.5
  281.5 0.0 copy-done.1
  281.5 2.8 fusion.1
  (4 shorter events, 0.0 us)
Async XLA Ops:
  149.4 3.6 %copy-start = (f32[2,8,9,128,128]{4,3,2,1,0:T(8,128)}, f32[2,8,9,128,128]{4,3,2,1,0:T(8,128)S(1)}, u32[]{:S(2)}) copy-start(f32[2,8,9,128,128]{4,3,2,1,0:T(8,128)S(1)} %get-tuple-element.11.lead_ref) | copy-start | bytes 28311556
  276.4 0.8 copy-start.2
  279.8 1.7 copy-start.1

commit v2 on v1

--- a/solution.py
+++ b/solution.py
@@ -81,7 +81,7 @@
     def block_of(i, k):
         apart = i - k
         source, slot = (i, apart) if 2 * apart <= count else (k, count - apart)
-        return lead_ref[source % 2, source // 2, slot]
+        return lead_ref[source % 2, (source // 2) * (count // 2 + 1) + slot]
 
     def given(r0, r1, k):
         lo = k * BLK
@@ -162,10 +162,12 @@
     uv_send, uv_recv, fw_send, fw_recv, cut_send, cut_recv, ring_send, ring_recv,
     flat_send, flat_recv, pair_send, pair_recv, vcut_send, vcut_recv, vflat_send, vflat_recv, local_sem,
 ):
-    rows, cols = flat_send.shape[0], vu_all.shape[0]
+    rows, cols = cut_send.shape[0], vu_all.shape[0]
+    side = {4: 2, 16: 4}[rows]
     depth = cols // 2
-    thin = piece.shape[2]
-    band = lead.shape[2]
+    band = cols // 2 + 1
+    slots = depth * band
+    thin = piece.shape[1]
     p, c = lax.axis_index("row"), lax.axis_index("col")
     z, core = c // 2, lax.rem(c, 2)
     sibling = c + 1 - 2 * core
@@ -173,8 +175,11 @@
     def along(d):
         return (p, 2 * lax.rem(z + d, depth) + core)
 
-    def plane(d):
-        return (lax.rem(p + d, rows), c)
+    def shift(q, axis, steps):
+        x, y = q // side, lax.rem(q, side)
+        if axis == 0:
+            return lax.rem(x + steps + side, side) * side + y
+        return x * side + lax.rem(y + steps + side, side)
 
     def remote(src, dst, send, recv, where):
         return pltpu.make_async_remote_copy(
@@ -183,7 +188,7 @@
         )
 
     barrier = pltpu.get_barrier_semaphore()
-    partners = [along(d) for d in range(1, depth)] + [(p, sibling)] + [plane(d) for d in range(1, rows)]
+    partners = [along(d) for d in range(1, depth)] + [(p, sibling)] + [(lax.rem(p + d, rows), c) for d in range(1, rows)]
     for where in partners:
         pl.semaphore_signal(barrier, inc=1, device_id=where, device_id_type=pl.DeviceIdType.MESH)
     pl.semaphore_wait(barrier, len(partners))
@@ -216,8 +221,9 @@
     first, own = spread_start(0)
     spread_end(0, first, own)
 
+    mine_slots = pl.ds(z * band, band)
     cuts = [
-        remote(blocks.at[:, pl.ds(d * thin, thin), :], piece.at[z], cut_send.at[d], cut_recv, (d, c))
+        remote(blocks.at[:, pl.ds(d * thin, thin), :], piece.at[mine_slots], cut_send.at[d], cut_recv, (d, c))
         for d in range(1, rows)
     ]
 
@@ -258,7 +264,7 @@
             @pl.when(c < j)
             def _(block=block, j=j):
                 blocks[j] = block.T
-        piece[z] = blocks[:, :thin, :]
+        piece[mine_slots] = blocks[:, :thin, :]
         for copy in cuts:
             copy.start()
 
@@ -268,28 +274,136 @@
 
     ring = []
     for d in range(1, depth):
-        copy = remote(piece.at[z], piece.at[z], ring_send.at[d], ring_recv.at[d], along(d))
+        copy = remote(piece.at[mine_slots], piece.at[mine_slots], ring_send.at[d], ring_recv.at[d], along(d))
         copy.start()
         ring.append(copy)
-    first, own = spread_start(1)
     for copy in ring:
         copy.wait_recv()
-
-    def place(q):
-        return lead.at[core, :, :, pl.ds(pl.multiple_of(q * thin, thin), thin), :]
-
-    flats = []
-    for d in range(1, rows):
-        copy = remote(piece, place(p), flat_send.at[d], flat_recv.at[d], plane(d))
-        copy.start()
-        flats.append(copy)
-    keep = pltpu.make_async_copy(piece, place(p), local_sem)
+    first, own = spread_start(1)
+
+    middle, quarter = slots // 2, slots // 4
+    edges = [(0, quarter, middle), (middle, middle + quarter, slots)]
+
+    def lead_region(q, k, part):
+        lo, mid, hi = edges[k]
+        lo, hi = {None: (lo, hi), 0: (lo, mid), 1: (mid, hi)}[part]
+        return lead.at[core, pl.ds(lo, hi - lo), pl.ds(pl.multiple_of(q * thin, thin), thin), :]
+
+    def piece_region(q, k, part):
+        lo, mid, hi = edges[k]
+        return piece.at[pl.ds(lo, hi - lo)]
+
+    def pair_region(q, k, part):
+        half = BLK // 2
+        lo, size = {None: (0, half), 0: (0, half // 2), 1: (half // 2, half // 2)}[part]
+        return vv_all.at[q, pl.ds(k * half + lo, size)]
+
+    def plane_gather(region, origin, send, recv, shared):
+        copies, siblings = [], []
+        ring_of = [(1 - k, k) for k in range(2)]
+
+        def go(k, slot, src, dst, axis, steps):
+            copy = remote(src, dst, send.at[k, slot], recv.at[k, slot], (shift(p, axis, steps), c))
+            copy.start()
+            copies.append(copy)
+            return copy
+
+        def share(k, q, index, src=None):
+            if shared is not None:
+                held = region(q, k, None)
+                copy = remote(held if src is None else src, held, shared[0].at[k, index], shared[1].at[k, index], (p, sibling))
+                copy.start()
+                siblings.append(copy)
+
+        units = {}
+        first_hop, second_hop = {}, {}
+
+        def fan(k, t, q, src=None):
+            axis = ring_of[k][1]
+            whole = region(q, k, None)
+            src = whole if src is None else src
+            units[k, t] = q
+            second_hop[k, t, 0] = go(k, 4 + 4 * t, src, whole, axis, 1)
+            if side == 4:
+                second_hop[k, t, 1] = go(k, 5 + 4 * t, src, whole, axis, -1)
+            share(k, q, 4 * t, src)
+
+        for k in range(2):
+            axis = ring_of[k][0]
+            src, whole = origin(p, k, None), region(p, k, None)
+            first_hop[k, 0] = go(k, 0, src, whole, axis, 1)
+            if side == 4:
+                first_hop[k, 1] = go(k, 1, src, whole, axis, -1)
+            fan(k, 0, p, src)
+        yield
+        for k in range(2):
+            axis = ring_of[k][0]
+            first_hop[k, 0].wait_recv()
+            q = shift(p, axis, -1)
+            if side == 4:
+                part = region(q, k, 0)
+                first_hop[k, 2] = go(k, 2, part, part, axis, 1)
+            fan(k, 1, q)
+        if side == 4:
+            for k in range(2):
+                axis = ring_of[k][0]
+                first_hop[k, 1].wait_recv()
+                q = shift(p, axis, 1)
+                part = region(q, k, 1)
+                first_hop[k, 3] = go(k, 3, part, part, axis, -1)
+                fan(k, 2, q)
+        yield
+
+        def relay(t):
+            for k in range(2):
+                axis = ring_of[k][1]
+                second_hop[k, t, 0].wait_recv()
+                q = shift(units[k, t], axis, -1)
+                if side == 4:
+                    part = region(q, k, 0)
+                    second_hop[k, t, 2] = go(k, 6 + 4 * t, part, part, axis, 1)
+                share(k, q, 4 * t + 1)
+                if side == 4:
+                    second_hop[k, t, 1].wait_recv()
+                    q = shift(units[k, t], axis, 1)
+                    part = region(q, k, 1)
+                    second_hop[k, t, 3] = go(k, 7 + 4 * t, part, part, axis, -1)
+                    share(k, q, 4 * t + 2)
+
+        relay(0)
+        if side == 4:
+            for k in range(2):
+                axis = ring_of[k][0]
+                first_hop[k, 2].wait_recv()
+                first_hop[k, 3].wait_recv()
+                fan(k, 3, shift(p, axis, 2))
+        yield
+        for t in range(1, side):
+            relay(t)
+        yield
+        if side == 4:
+            for t in range(side):
+                for k in range(2):
+                    axis = ring_of[k][1]
+                    second_hop[k, t, 2].wait_recv()
+                    second_hop[k, t, 3].wait_recv()
+                    share(k, shift(units[k, t], axis, 2), 4 * t + 3)
+        yield
+        for copy in siblings:
+            copy.wait_recv()
+        for copy in copies + siblings:
+            copy.wait_send()
+        yield
+
+    keep = pltpu.make_async_copy(piece, lead.at[core, :, pl.ds(pl.multiple_of(p * thin, thin), thin), :], local_sem)
     keep.start()
-    halfway = [remote(piece, place(p), pair_send.at[0], pair_recv.at[0], (p, sibling))]
-    halfway[0].start()
+    lead_gather = plane_gather(lead_region, piece_region, flat_send, flat_recv, (pair_send, pair_recv))
+    next(lead_gather)
+    next(lead_gather)
+    next(lead_gather)
 
     spread_end(1, first, own)
-    vcuts = [remote(pairs.at[d], vv_all.at[lax.rem(p + d, rows)], vcut_send.at[d], vcut_recv, plane(d)) for d in range(1, rows)]
+    vcuts = [remote(pairs.at[d], vv_all.at[lax.rem(p + d, rows)], vcut_send.at[d], vcut_recv, (lax.rem(p + d, rows), c)) for d in range(1, rows)]
 
     @pl.when(p == c)
     def _():
@@ -303,26 +417,23 @@
         for copy in vcuts:
             copy.start()
 
+    next(lead_gather)
+
     @pl.when(p != c)
     def _():
         vcuts[0].wait_recv()
 
-    vflats = []
-    for d in range(1, rows):
-        copy = remote(vv_all.at[p], vv_all.at[p], vflat_send.at[d], vflat_recv.at[d], plane(d))
-        copy.start()
-        vflats.append(copy)
-
-    for d in range(1, rows):
-        flats[d - 1].wait_recv()
-        held = place(lax.rem(p + rows - d, rows))
-        copy = remote(held, held, pair_send.at[d], pair_recv.at[d], (p, sibling))
-        copy.start()
-        halfway.append(copy)
+    pair_gather = plane_gather(pair_region, pair_region, vflat_send, vflat_recv, None)
+    next(pair_gather)
+    next(pair_gather)
+    next(pair_gather)
+    next(lead_gather)
+    next(pair_gather)
+    next(pair_gather)
+    next(lead_gather)
+    next(pair_gather)
     keep.wait()
-    for copy in halfway + vflats:
-        copy.wait_recv()
-    for copy in pending + ring + flats + halfway + vflats:
+    for copy in pending + ring:
         copy.wait_send()
 
     @pl.when(p == 0)
@@ -345,20 +456,20 @@
         exchange_kernel,
         out_shape=(
             jax.ShapeDtypeStruct((cols, 2, BLK, BLK), jnp.bfloat16),
-            jax.ShapeDtypeStruct((cols, BLK, BLK), jnp.bfloat16),
-            jax.ShapeDtypeStruct((2, depth, band, BLK, BLK), jnp.float32),
+            jax.ShapeDtypeStruct((rows, BLK, BLK), jnp.bfloat16),
+            jax.ShapeDtypeStruct((2, depth * band, BLK, BLK), jnp.float32),
         ),
         in_specs=[vm, vm],
         out_specs=(vm, vm, pl.BlockSpec(memory_space=pl.ANY)),
         scratch_shapes=[
             pltpu.VMEM((band, BLK, BLK), jnp.float32),
-            pltpu.VMEM((depth, band, thin, BLK), jnp.float32),
-            pltpu.VMEM((cols, BLK, BLK), jnp.bfloat16),
+            pltpu.VMEM((depth * band, thin, BLK), jnp.float32),
+            pltpu.VMEM((rows, BLK, BLK), jnp.bfloat16),
             pltpu.VMEM((cols, BLK, BLK), jnp.bfloat16),
             dma((2, depth)), dma((2, depth)), dma((2, depth)), dma((2, depth)),
             dma((rows,)), dma, dma((depth,)), dma((depth,)),
-            dma((rows,)), dma((rows,)), dma((rows,)), dma((rows,)),
-            dma((rows,)), dma, dma((rows,)), dma((rows,)), dma,
+            dma((2, 20)), dma((2, 20)), dma((2, 16)), dma((2, 16)),
+            dma((rows,)), dma, dma((2, 20)), dma((2, 20)), dma,
         ],
         compiler_params=pltpu.CompilerParams(
             collective_id=0, has_side_effects=True, vmem_limit_bytes=40 * 2**20

time: 285 us -> 223 us (0.78)
  the two profiles are of different devices: /device:TPU:192 before, /device:TPU:130 now
where the time goes in v2:
time: 223 us
  Pallas kernels  205 us (92%)
  local copies, waits for them, and re-layouts  8.17 us (4%)
  matrix products  6.41 us (3%)
  other arithmetic  3.03 us (1%)
    pallas_call x1, Pallas kernels, chol_call(): pl.pallas_call(chol_kernel, out_shape=(jax.ShapeDtypeStruct((count, order...  123 us
    pallas_call x1, Pallas kernels, exchange(): pl.pallas_call(exchange_kernel, out_shape=(jax.ShapeDtypeStruct((cols, 2,...  81.2 us
    unnamed x8, local copies, waits for them, and re-layouts  5.43 us

profile of v2, /device:TPU:130, one launch (start us, length us, event | category | flops | bytes accessed | tf_op | source)
XLA Modules:
  0.0 222.9 jit_solution(16580086018086309831)
XLA Ops:
  0.6 0.6 pad_add_fusion.pos_ref
  1.2 0.1 broadcast_compare_fusion
  1.3 0.8 and_select_fusion
  2.2 0.9 copy.17
  3.1 0.9 copy.16
  3.9 0.8 fusion.17
  4.7 0.1 maximum_bitcast_fusion.vu_ref
  4.8 0.7 pad_convert_fusion.y_ref
  5.5 1.3 slice_bitcast_fusion.diag_ref
  6.8 81.2 %shard_map.93 = (bf16[16,2,128,128]{3,2,1,0:T(8,128)(2,1)S(1)}, bf16[16,128,128]{2,1,0:T(8,128)(2,1)S(1)}, f32[2,72,128,128]{3,2,1,0:T(8,128)S(1)}) custom-call(bf16[2,128,128]{2,1,0:T(8,128)(2,1)S(1)} %maximum_bitcast_fusion.vu_ref, f32[128,2048]{1,0:T(8,128)S(1)} %slice_bitcast_fusion.diag_ref), custom_call_target="tpu_custom_call" | custom-call | tf_op jit(solution)/shard_map/pallas_call | solution.py:455
  88.0 0.0 copy-start
  88.0 3.6 %copy-done = f32[2,72,128,128]{3,2,1,0:T(8,128)} copy-done((f32[2,72,128,128]{3,2,1,0:T(8,128)}, f32[2,72,128,128]{3,2,1,0:T(8,128)S(1)}, u32[]{:S(2)}) %copy-start) | copy-done | bytes 9437208
  91.6 123.4 %shard_map.94 = (f32[8,2048]{1,0:T(8,128)}, f32[128,128]{1,0:T(8,128)}) custom-call(s32[2]{0:T(128)} %pad_add_fusion.pos_ref, f32[2,72,128,128]{3,2,1,0:T(8,128)} %copy-done, f32[16,2048]{1,0:T(8,128)} %pad_convert_fusion.y_ref), custom_call_target="tpu_custom_call" | custom-call | flops 99999997952 | bytes 200000000 | tf_op jit(solution)/shard_map/pallas_call | solution.py:142
  215.0 0.0 copy-start.2
  215.0 0.4 copy.18
  215.5 0.2 reshape.76
  215.7 0.1 copy.19
  215.8 0.1 copy-done.2
  215.9 0.7 reshape.75
  216.5 1.9 fusion.3
  218.4 0.0 copy-start.1
  218.4 1.7 fusion.5
  220.1 0.0 copy-done.1
  220.1 2.8 %fusion.1 = f32[2,1,128,2048]{3,2,1,0:T(8,128)} fusion(f32[2,1,128,2048]{3,2,1,0:T(8,128)S(1)} %copy-done.1, bf16[2,2048,128]{2,1,0:T(8,128)(2,1)S(1)} %bitcast.49, bf16[2,2048,64]{1,2,0:T(8,128)(2,1)} %fusion.5, s32[]{:T(128)S(6)} %select_n.22), kind=kOutput, calls=%fused_computation.3 | convolution fusion | flops 67633152 | bytes 5275652 | tf_op jit(solution)/shard_map/ans,ams->anm/dot_general | solution.py:507
  (4 shorter events, 0.0 us)
Async XLA Ops:
  88.0 3.6 %copy-start = (f32[2,72,128,128]{3,2,1,0:T(8,128)}, f32[2,72,128,128]{3,2,1,0:T(8,128)S(1)}, u32[]{:S(2)}) copy-start(f32[2,72,128,128]{3,2,1,0:T(8,128)S(1)} %get-tuple-element.11.lead_ref) | copy-start | bytes 28311556
  215.0 0.8 copy-start.2
  218.4 1.7 copy-start.1

commit v3 on v2

--- a/solution.py
+++ b/solution.py
@@ -13,46 +13,74 @@
 
 def invert_factor(rows):
     count = len(rows)
-    lanes = lax.broadcasted_iota(jnp.int32, (GRP, BLK), 1)
-    subs = lax.broadcasted_iota(jnp.int32, (GRP, BLK), 0)
     shape = (GRP, BLK)
-    rows = list(rows)
+    lanes = lax.broadcasted_iota(jnp.int32, shape, 1)
+    subs = lax.broadcasted_iota(jnp.int32, shape, 0)
+
+    def lane(value, index):
+        return jnp.broadcast_to(value[:, index : index + 1], shape)
+
+    def line(value, index):
+        return jnp.broadcast_to(value[index : index + 1, :], shape)
+
+    kept = [jnp.where(lanes == subs + g * GRP, rows[g], 0.0) for g in range(count)]
+    tall = [lax.rsqrt(jnp.broadcast_to(jnp.sum(k, axis=1, keepdims=True), shape)) for k in kept]
+    total = kept[0]
+    for g in range(1, count):
+        total = total + kept[g]
+    wide = lax.rsqrt(jnp.broadcast_to(jnp.sum(total, axis=0, keepdims=True), shape))
+    rows = [rows[g] * tall[g] * wide for g in range(count)]
+
     out = []
+    edge = [lane(rows[0], k) for k in range(GRP)]
     for g in range(count):
         base = g * GRP
         here = (lanes >= base) & (lanes < base + GRP)
-        cols = {
-            h: [jnp.broadcast_to(rows[h][:, base + j : base + j + 1], shape) for j in range(GRP)]
-            for h in range(g, count)
-        }
-        tri = {
-            (i, j): jnp.broadcast_to(cols[g][j][i : i + 1, :], shape)
-            for j in range(GRP)
-            for i in range(j, GRP)
-        }
+        last = g + 1 == count
+        tri = {(i, j): line(edge[j], i) for j in range(GRP) for i in range(j, GRP)}
+        cols = {h: [lane(rows[h], base + j) for j in range(GRP)] for h in range(g + 1, count)}
+        if not last:
+            near = list(cols[g + 1])
+            edge = [lane(rows[g + 1], base + GRP + k) for k in range(GRP)]
         pivot = jnp.where(here, jnp.where(lanes - base == subs, 1.0, 0.0), rows[g])
-        lines = [jnp.broadcast_to(pivot[j : j + 1, :], shape) for j in range(GRP)]
-        inv = []
-        unit = {}
-        for j in range(GRP):
-            inv.append(recip(tri[j, j]))
-            for i in range(j + 1, GRP):
-                unit[i, j] = tri[i, j] * inv[j]
-            for i in range(j + 1, GRP):
-                for k in range(j + 1, i + 1):
-                    tri[i, k] = tri[i, k] - unit[i, j] * tri[k, j]
-                lines[i] = lines[i] - unit[i, j] * lines[j]
-        done = lines[0] * lax.rsqrt(tri[0, 0])
-        for j in range(1, GRP):
-            done = jnp.where(subs == j, lines[j] * lax.rsqrt(tri[j, j]), done)
-        out.append(jnp.where(lanes <= subs + base, done, 0.0))
-        if g + 1 < count:
+        lines = [line(pivot, j) for j in range(GRP)]
+        weight = {}
+        pairs = []
+        done = jnp.zeros(shape, jnp.float32)
+        for j in range(0, GRP, 2):
+            a, b, c = tri[j, j], tri[j + 1, j], tri[j + 1, j + 1]
+            det = a * c - b * b
+            r = recip(det)
+            pairs.append((a, b, c, r))
+            for i in range(j + 2, GRP):
+                x, y = tri[i, j], tri[i, j + 1]
+                u, v = c * x - b * y, a * y - b * x
+                for k in range(j + 2, i + 1):
+                    tri[i, k] = tri[i, k] - r * (u * tri[k, j] + v * tri[k, j + 1])
+                weight[i, j], weight[i, j + 1] = u * r, v * r
+                lines[i] = lines[i] - (weight[i, j] * lines[j] + weight[i, j + 1] * lines[j + 1])
+            if not last:
+                u = c * near[j] - b * near[j + 1]
+                v = a * near[j + 1] - b * near[j]
+                for k in range(GRP):
+                    edge[k] = edge[k] - r * (u * line(near[j], k) + v * line(near[j + 1], k))
+                for k in range(j + 2, GRP):
+                    near[k] = near[k] - r * (u * tri[k, j] + v * tri[k, j + 1])
+            root = lax.rsqrt(a)
+            done = jnp.where(subs == j, lines[j] * root, done)
+            second = (lines[j + 1] - (b * root * root) * lines[j]) * (a * root * lax.rsqrt(det))
+            done = jnp.where(subs == j + 1, second, done)
+        out.append(jnp.where(lanes <= subs + base, done, 0.0) * wide)
+        if not last:
             back = [None] * GRP
-            for j in range(GRP - 1, -1, -1):
-                acc = lines[j] * inv[j]
-                for i in range(GRP - 1, j, -1):
-                    acc = acc - unit[i, j] * back[i]
-                back[j] = acc
+            for j in range(GRP - 2, -1, -2):
+                a, b, c, r = pairs[j // 2]
+                first = r * (c * lines[j] - b * lines[j + 1])
+                second = r * (a * lines[j + 1] - b * lines[j])
+                for i in range(GRP - 1, j + 1, -1):
+                    first = first - weight[i, j] * back[i]
+                    second = second - weight[i, j + 1] * back[i]
+                back[j], back[j + 1] = first, second
             for h in range(g + 1, count):
                 acc = jnp.where(here, 0.0, rows[h])
                 for j in range(GRP - 1, -1, -1):
@@ -79,6 +107,8 @@
     row, col = pos_ref[0], pos_ref[1]
 
     def block_of(i, k):
+        if i < k:
+            return jnp.zeros((BLK, BLK), jnp.float32)
         apart = i - k
         source, slot = (i, apart) if 2 * apart <= count else (k, count - apart)
         return lead_ref[source % 2, (source // 2) * (count // 2 + 1) + slot]
@@ -90,17 +120,22 @@
             parts.append(y_ref[max(r0, order) - order:r1 - order, lo:lo + BLK])
         return parts[0] if len(parts) == 1 else jnp.concatenate(parts, axis=0)
 
-    for r in range(0, order, BLK):
-        work[r:r + BLK, :] = block_of(r // BLK, 0)
-    work[order:, :] = y_ref[:, :BLK]
+    def pair_given(r0, r1, k):
+        if k + 1 == count:
+            return given(r0, r1, k)
+        return jnp.concatenate([given(r0, r1, k), given(r0, r1, k + 1)], axis=1)
+
+    def spans(start, size):
+        return [(r, min(r + size, total)) for r in range(start, total, size)]
+
+    for r0, r1 in spans(0, 2 * BLK):
+        work[r0:r1, :] = pair_given(r0, r1, 0)
     part_ref[...] = jnp.zeros_like(part_ref)
-
-    def spans(start):
-        return [(r, min(r + 2 * BLK, total)) for r in range(start, total, 2 * BLK)]
 
     def step(k, carry):
         base = pl.multiple_of(k * BLK, BLK)
-        rows = [work[pl.ds(base + g * GRP, GRP), :] for g in range(BLK // GRP)]
+        side = pl.ds(pl.multiple_of(lax.rem(k, 2) * BLK, BLK), BLK)
+        rows = [work[pl.ds(base + g * GRP, GRP), side] for g in range(BLK // GRP)]
         inverse = invert_factor(rows)
         full = jnp.concatenate(inverse, axis=0)
         high_part, low_part = halves(full)
@@ -111,27 +146,34 @@
             @pl.when(k == s)
             def _(s=s):
                 lo, hi = s * BLK, s * BLK + BLK
-                for r0, r1 in spans(lo):
-                    sh, sl = halves(work[r0:r1, :])
+                left = (s % 2) * BLK
+                for r0, r1 in spans(lo, 4 * BLK):
+                    sh, sl = halves(work[r0:r1, left:left + BLK])
                     panel = mul3(sh, sl, wh[...], wl[...])
                     ph, pl_ = halves(panel)
                     high[r0:r1, lo:hi] = ph
                     low[r0:r1, lo:hi] = pl_
-                    work[r0:r1, :] = panel
-                x_ref[:, lo:hi] = work[order:order + x_ref.shape[0], :]
+                    work[r0:r1, left:left + BLK] = panel
+                x_ref[:, lo:hi] = work[order:order + x_ref.shape[0], left:left + BLK]
 
                 @pl.when(jnp.logical_and(col == s, row >= s))
                 def _():
-                    block = work[pl.ds(pl.multiple_of(row * BLK, BLK), BLK), :]
+                    block = work[pl.ds(pl.multiple_of(row * BLK, BLK), BLK), left:left + BLK]
                     r = lax.broadcasted_iota(jnp.int32, (BLK, BLK), 0)
                     c = lax.broadcasted_iota(jnp.int32, (BLK, BLK), 1)
                     part_ref[...] = jnp.where((row > s) | (r >= c), block, 0.0)
 
-                if s + 1 < count:
-                    for r0, r1 in spans(hi):
-                        work[r0:r1, :] = given(r0, r1, s + 1) - mul3(
+                if s % 2 == 0 and s + 1 < count:
+                    for r0, r1 in spans(hi, 4 * BLK):
+                        work[r0:r1, BLK:] = work[r0:r1, BLK:] - mul3(
+                            high[r0:r1, lo:hi], low[r0:r1, lo:hi],
+                            high[hi:hi + BLK, lo:hi], low[hi:hi + BLK, lo:hi])
+                if s % 2 == 1 and s + 1 < count:
+                    end = min(hi + 2 * BLK, order)
+                    for r0, r1 in spans(hi, 4 * BLK):
+                        work[r0:r1, :end - hi] = pair_given(r0, r1, s + 1) - mul3(
                             high[r0:r1, :hi], low[r0:r1, :hi],
-                            high[hi:hi + BLK, :hi], low[hi:hi + BLK, :hi])
+                            high[hi:end, :hi], low[hi:end, :hi])
         return carry
 
     lax.fori_loop(0, count, step, 0)
@@ -147,7 +189,7 @@
         scratch_shapes=[
             pltpu.VMEM((order + extra, order), jnp.bfloat16),
             pltpu.VMEM((order + extra, order), jnp.bfloat16),
-            pltpu.VMEM((order + extra, BLK), jnp.float32),
+            pltpu.VMEM((order + extra, 2 * BLK), jnp.float32),
             pltpu.VMEM((BLK, BLK), jnp.bfloat16),
             pltpu.VMEM((BLK, BLK), jnp.bfloat16),
         ],

time: 223 us -> 183 us (0.82)
  Pallas kernels: 205 us -> 164 us
    pallas_call x1, Pallas kernels: 123 us -> 82.5 us  [chol_call(): pl.pallas_call(chol_kernel, out_shape=(jax.ShapeDtypeStruct((count, order...]
where the time goes in v3:
time: 183 us; the launch traced here: 182 us
  Pallas kernels  164 us (90%)
  local copies, waits for them, and re-layouts  8.17 us (4%)
  matrix products  6.41 us (4%)
  other arithmetic  3.03 us (2%)
    pallas_call x1, Pallas kernels, chol_call(): pl.pallas_call(chol_kernel, out_shape=(jax.ShapeDtypeStruct((count, order...  82.5 us
    pallas_call x1, Pallas kernels, exchange(): pl.pallas_call(exchange_kernel, out_shape=(jax.ShapeDtypeStruct((cols, 2,...  81.2 us
    unnamed x8, local copies, waits for them, and re-layouts  5.43 us

profile of v3, /device:TPU:130, one launch (start us, length us, event | category | flops | bytes accessed | tf_op | source)
XLA Modules:
  0.0 182.1 jit_solution(3383992555345762850)
XLA Ops:
  0.6 0.6 pad_add_fusion.pos_ref
  1.2 0.1 broadcast_compare_fusion
  1.3 0.8 and_select_fusion
  2.2 0.9 copy.17
  3.1 0.9 copy.16
  3.9 0.8 fusion.17
  4.7 0.1 maximum_bitcast_fusion.vu_ref
  4.8 0.7 pad_convert_fusion.y_ref
  5.5 1.3 slice_bitcast_fusion.diag_ref
  6.8 81.2 %shard_map.93 = (bf16[16,2,128,128]{3,2,1,0:T(8,128)(2,1)S(1)}, bf16[16,128,128]{2,1,0:T(8,128)(2,1)S(1)}, f32[2,72,128,128]{3,2,1,0:T(8,128)S(1)}) custom-call(bf16[2,128,128]{2,1,0:T(8,128)(2,1)S(1)} %maximum_bitcast_fusion.vu_ref, f32[128,2048]{1,0:T(8,128)S(1)} %slice_bitcast_fusion.diag_ref), custom_call_target="tpu_custom_call" | custom-call | tf_op jit(solution)/shard_map/pallas_call | solution.py:497
  88.0 0.0 copy-start
  88.0 3.6 %copy-done = f32[2,72,128,128]{3,2,1,0:T(8,128)} copy-done((f32[2,72,128,128]{3,2,1,0:T(8,128)}, f32[2,72,128,128]{3,2,1,0:T(8,128)S(1)}, u32[]{:S(2)}) %copy-start) | copy-done | bytes 9437208
  91.6 82.5 %shard_map.94 = (f32[8,2048]{1,0:T(8,128)}, f32[128,128]{1,0:T(8,128)}) custom-call(s32[2]{0:T(128)} %pad_add_fusion.pos_ref, f32[2,72,128,128]{3,2,1,0:T(8,128)} %copy-done, f32[16,2048]{1,0:T(8,128)} %pad_convert_fusion.y_ref), custom_call_target="tpu_custom_call" | custom-call | flops 99999997952 | bytes 200000000 | tf_op jit(solution)/shard_map/pallas_call | solution.py:184
  174.2 0.0 copy-start.2
  174.2 0.4 copy.18
  174.6 0.2 reshape.76
  174.8 0.1 copy.19
  174.9 0.1 copy-done.2
  175.0 0.7 reshape.75
  175.7 1.9 %fusion.3 = bf16[2,1,2,1,2048,64]{4,5,3,2,1,0:T(8,128)(2,1)} fusion(bf16[2048,2,64,1]{0,2,1,3:T(8,128)(2,1)S(1)} %reshape.76, pred[2,2]{1,0:T(4,128)(4,1)S(1)} %broadcast_compare_fusion, bf16[2,2048,128]{2,1,0:T(8,128)(2,1)S(1)} %bitcast.47), kind=kOutput, calls=%fused_computation.5 | convolution fusion | flops 135282688 | bytes 3670528 | tf_op jit(solution)/shard_map/anr,abrs->abns/dot_general | solution.py:569
  177.6 0.0 copy-start.1
  177.6 1.7 fusion.5
  179.3 0.0 copy-done.1
  179.3 2.8 %fusion.1 = f32[2,1,128,2048]{3,2,1,0:T(8,128)} fusion(f32[2,1,128,2048]{3,2,1,0:T(8,128)S(1)} %copy-done.1, bf16[2,2048,128]{2,1,0:T(8,128)(2,1)S(1)} %bitcast.49, bf16[2,2048,64]{1,2,0:T(8,128)(2,1)} %fusion.5, s32[]{:T(128)S(6)} %select_n.22), kind=kOutput, calls=%fused_computation.3 | convolution fusion | flops 67633152 | bytes 5275652 | tf_op jit(solution)/shard_map/ans,ams->anm/dot_general | solution.py:549
  (4 shorter events, 0.0 us)
Async XLA Ops:
  88.0 3.6 %copy-start = (f32[2,72,128,128]{3,2,1,0:T(8,128)}, f32[2,72,128,128]{3,2,1,0:T(8,128)S(1)}, u32[]{:S(2)}) copy-start(f32[2,72,128,128]{3,2,1,0:T(8,128)S(1)} %get-tuple-element.11.lead_ref) | copy-start | bytes 28311556
  174.2 0.8 copy-start.2
  177.6 1.7 copy-start.1

commit v4 on v0

v4 whole, which is shorter than its diff:
```python
import jax, jax.numpy as jnp
from jax import lax
from jax.sharding import PartitionSpec as P
from jax.experimental import pallas as pl
from jax.experimental.pallas import tpu as pltpu

BLK = 128
GRP = 8

def recip(value):
    start = pl.reciprocal(value, approx=True)
    return start * (2.0 - value * start)

def invert_factor(rows):
    count = len(rows)
    shape = (GRP, BLK)
    lanes = lax.broadcasted_iota(jnp.int32, shape, 1)
    subs = lax.broadcasted_iota(jnp.int32, shape, 0)

    def lane(value, index):
        return jnp.broadcast_to(value[:, index : index + 1], shape)

    def line(value, index):
        return jnp.broadcast_to(value[index : index + 1, :], shape)

    kept = [jnp.where(lanes == subs + g * GRP, rows[g], 0.0) for g in range(count)]
    tall = [lax.rsqrt(jnp.broadcast_to(jnp.sum(k, axis=1, keepdims=True), shape)) for k in kept]
    total = kept[0]
    for g in range(1, count):
        total = total + kept[g]
    wide = lax.rsqrt(jnp.broadcast_to(jnp.sum(total, axis=0, keepdims=True), shape))
    rows = [rows[g] * tall[g] * wide for g in range(count)]

    out = []
    edge = [lane(rows[0], k) for k in range(GRP)]
    for g in range(count):
        base = g * GRP
        here = (lanes >= base) & (lanes < base + GRP)
        last = g + 1 == count
        tri = {(i, j): line(edge[j], i) for j in range(GRP) for i in range(j, GRP)}
        cols = {h: [lane(rows[h], base + j) for j in range(GRP)] for h in range(g + 1, count)}
        if not last:
            near = list(cols[g + 1])
            edge = [lane(rows[g + 1], base + GRP + k) for k in range(GRP)]
        pivot = jnp.where(here, jnp.where(lanes - base == subs, 1.0, 0.0), rows[g])
        lines = [line(pivot, j) for j in range(GRP)]
        weight = {}
        pairs = []
        done = jnp.zeros(shape, jnp.float32)
        for j in range(0, GRP, 2):
            a, b, c = tri[j, j], tri[j + 1, j], tri[j + 1, j + 1]
            det = a * c - b * b
            r = recip(det)
            pairs.append((a, b, c, r))
            for i in range(j + 2, GRP):
                x, y = tri[i, j], tri[i, j + 1]
                u, v = c * x - b * y, a * y - b * x
                for k in range(j + 2, i + 1):
                    tri[i, k] = tri[i, k] - r * (u * tri[k, j] + v * tri[k, j + 1])
                weight[i, j], weight[i, j + 1] = u * r, v * r
                lines[i] = lines[i] - (weight[i, j] * lines[j] + weight[i, j + 1] * lines[j + 1])
            if not last:
                u = c * near[j] - b * near[j + 1]
                v = a * near[j + 1] - b * near[j]
                for k in range(GRP):
                    edge[k] = edge[k] - r * (u * line(near[j], k) + v * line(near[j + 1], k))
                for k in range(j + 2, GRP):
                    near[k] = near[k] - r * (u * tri[k, j] + v * tri[k, j + 1])
            root = lax.rsqrt(a)
            done = jnp.where(subs == j, lines[j] * root, done)
            second = (lines[j + 1] - (b * root * root) * lines[j]) * (a * root * lax.rsqrt(det))
            done = jnp.where(subs == j + 1, second, done)
        out.append(jnp.where(lanes <= subs + base, done, 0.0) * wide)
        if not last:
            back = [None] * GRP
            for j in range(GRP - 2, -1, -2):
                a, b, c, r = pairs[j // 2]
                first = r * (c * lines[j] - b * lines[j + 1])
                second = r * (a * lines[j + 1] - b * lines[j])
                for i in range(GRP - 1, j + 1, -1):
                    first = first - weight[i, j] * back[i]
                    second = second - weight[i, j + 1] * back[i]
                back[j], back[j + 1] = first, second
            for h in range(g + 1, count):
                acc = jnp.where(here, 0.0, rows[h])
                for j in range(GRP - 1, -1, -1):
                    acc = acc - cols[h][j] * back[j]
                rows[h] = acc
    return out

NT = (((1,), (1,)), ((), ()))

def halves(value):
    high = value.astype(jnp.bfloat16)
    return high, (value - high.astype(jnp.float32)).astype(jnp.bfloat16)

def mul3(lh, ll, rh, rl):
    def one(x, y):
        return lax.dot_general(x, y, NT, preferred_element_type=jnp.float32)
    return one(lh, rh) + (one(lh, rl) + one(ll, rh))

MESH = pl.DeviceIdType.MESH


def lead_place(i, k, count):
    first = early_count(count)
    if k < first:
        return 0, i, k
    apart, ring = i - k, count - first
    source, slot = (i, apart) if 2 * apart <= ring else (k, ring - apart)
    return 1, source, slot


def early_count(count):
    return max(2, count // 4)


def update_kernel(
    vu_ref, diag_ref, y_ref,
    vu_all, vv_all, x_ref, part_ref,
    lead_a, lead_b, blocks_a, blocks_b, piece_a, piece_b, pairs, um, own_mu, high, low, work, wh, wl,
    uv_send, uv_recv, fw_send, fw_recv, cut_send, cut_recv, ring_send, ring_recv,
    flat_send, flat_recv, pair_send, pair_recv, vcut_send, vcut_recv, vflat_send, vflat_recv, local_sem,
):
    rows, cols = cut_send.shape[1], vu_all.shape[0]
    side = {4: 2, 16: 4}[rows]
    depth = cols // 2
    early = early_count(cols)
    late = cols - early
    thin = piece_a.shape[1]
    p, c = lax.axis_index("row"), lax.axis_index("col")
    z, core = c // 2, lax.rem(c, 2)
    sibling = c + 1 - 2 * core

    order = y_ref.shape[1]
    count = cols
    total = order + y_ref.shape[0]

    def along(d):
        return (p, 2 * lax.rem(z + d, depth) + core)

    def shift(q, axis, steps):
        x, y = q // side, lax.rem(q, side)
        if axis == 0:
            return lax.rem(x + steps + side, side) * side + y
        return x * side + lax.rem(y + steps + side, side)

    def remote(src, dst, send, recv, where):
        return pltpu.make_async_remote_copy(
            src_ref=src, dst_ref=dst, send_sem=send, recv_sem=recv, device_id=where, device_id_type=MESH
        )

    def start_all(copies):
        for copy in copies:
            copy.start()

    barrier = pltpu.get_barrier_semaphore()
    partners = [along(d) for d in range(1, depth)] + [(p, sibling)] + [(lax.rem(p + d, rows), c) for d in range(1, rows)]
    for where in partners:
        pl.semaphore_signal(barrier, inc=1, device_id=where, device_id_type=MESH)
    pl.semaphore_wait(barrier, len(partners))

    spreads = []
    for a in range(2):
        first = [
            remote(vu_ref.at[a], vu_all.at[c, a], uv_send.at[a, d], uv_recv.at[a, d], along(d)) for d in range(1, depth)
        ]
        held = [vu_all.at[2 * lax.rem(z + depth - d, depth) + core, a] for d in range(depth)]
        later = [remote(vu_ref.at[a], vu_all.at[c, a], fw_send.at[a, 0], fw_recv.at[a, 0], (p, sibling))] + [
            remote(held[d], held[d], fw_send.at[a, d], fw_recv.at[a, d], (p, sibling)) for d in range(1, depth)
        ]
        spreads.append((first, later))

    def spread_start(a):
        first, later = spreads[a]
        start_all(first)
        later[0].start()
        vu_all[c, a] = vu_ref[a]

    def spread_pass(a):
        first, later = spreads[a]
        for one, two in zip(first, later[1:]):
            one.wait_recv()
            two.start()

    def spread_end(a):
        for copy in spreads[a][1]:
            copy.wait_recv()

    phases = []
    for f, (blocks, piece) in enumerate(((blocks_a, piece_a), (blocks_b, piece_b))):
        wide = blocks.shape[0]
        mine = piece.at[pl.ds(z * wide, wide)]
        cuts = [
            remote(blocks.at[:, pl.ds(d * thin, thin), :], mine, cut_send.at[f, d], cut_recv.at[f], (d, c))
            for d in range(1, rows)
        ]
        ring = [remote(mine, mine, ring_send.at[f, d], ring_recv.at[f, d], along(d)) for d in range(1, depth)]
        phases.append((cuts, ring, mine))

    def plane_gather(region, origin, send, recv, shared):
        hops, shares = {}, {}
        units = {}

        def add(k, slot, src, dst, axis, steps):
            hops[k, slot] = remote(src, dst, send.at[k, slot], recv.at[k, slot], (shift(p, axis, steps), c))

        def share(k, index, q, src=None):
            if shared is not None:
                held = region(q, k, None)
                shares[k, index] = remote(
                    held if src is None else src, held, shared[0].at[k, index], shared[1].at[k, index], (p, sibling)
                )

        for k in range(2):
            one, two = 1 - k, k
            src, whole = origin(k), region(p, k, None)
            add(k, 0, src, whole, one, 1)
            if side == 4:
                add(k, 1, src, whole, one, -1)
                back, ahead = region(shift(p, one, -1), k, 0), region(shift(p, one, 1), k, 1)
                add(k, 2, back, back, one, 1)
                add(k, 3, ahead, ahead, one, -1)
            steps = (0, -1, 1, 2)[:side]
            for t, step in enumerate(steps):
                q = shift(p, one, step) if step else p
                whole = region(q, k, None)
                src = origin(k) if t == 0 else whole
                add(k, 4 + 4 * t, src, whole, two, 1)
                share(k, 4 * t, q, src)
                share(k, 4 * t + 1, shift(q, two, -1))
                if side == 4:
                    add(k, 5 + 4 * t, src, whole, two, -1)
                    back, ahead = region(shift(q, two, -1), k, 0), region(shift(q, two, 1), k, 1)
                    add(k, 6 + 4 * t, back, back, two, 1)
                    add(k, 7 + 4 * t, ahead, ahead, two, -1)
                    share(k, 4 * t + 2, shift(q, two, 1))
                    share(k, 4 * t + 3, shift(q, two, 2))

        def go(k, slot):
            if (k, slot) in hops:
                hops[k, slot].start()

        def arrived(k, slot):
            if (k, slot) in hops:
                hops[k, slot].wait_recv()

        def hand(k, index):
            if (k, index) in shares:
                shares[k, index].start()

        def fan(k, t):
            go(k, 4 + 4 * t)
            go(k, 5 + 4 * t)
            hand(k, 4 * t)

        def relay(t):
            for k in range(2):
                arrived(k, 4 + 4 * t)
                go(k, 6 + 4 * t)
                hand(k, 4 * t + 1)
                arrived(k, 5 + 4 * t)
                go(k, 7 + 4 * t)
                hand(k, 4 * t + 2)

        def stage(number):
            if number == 0:
                for k in range(2):
                    go(k, 0)
                    go(k, 1)
                    fan(k, 0)
            if number == 1:
                for k in range(2):
                    arrived(k, 0)
                    go(k, 2)
                    fan(k, 1)
                if side == 4:
                    for k in range(2):
                        arrived(k, 1)
                        go(k, 3)
                        fan(k, 2)
            if number == 2:
                relay(0)
                if side == 4:
                    for k in range(2):
                        arrived(k, 2)
                        arrived(k, 3)
                        fan(k, 3)
            if number == 3:
                for t in range(1, side):
                    relay(t)
            if number == 4 and side == 4:
                for t in range(side):
                    for k in range(2):
                        arrived(k, 6 + 4 * t)
                        arrived(k, 7 + 4 * t)
                        hand(k, 4 * t + 3)
            if number == 5:
                for copy in shares.values():
                    copy.wait_recv()
            if number == 6:
                for copy in list(hops.values()) + list(shares.values()):
                    copy.wait_send()

        return stage

    def lead_stages(f, lead, piece, skip):
        slots = lead.shape[1]
        middle, quarter = slots // 2, slots // 4
        edges = [(0, quarter, middle), (middle, middle + quarter, slots)]

        def region(q, k, part):
            lo, mid, hi = edges[k]
            lo, hi = {None: (lo, hi), 0: (lo, mid), 1: (mid, hi)}[part]
            return lead.at[core, pl.ds(lo, hi - lo), pl.ds(pl.multiple_of(q * thin, thin), thin), :]

        def origin(k):
            lo, mid, hi = edges[k]
            return piece.at[pl.ds(skip + lo, hi - lo)]

        stage = plane_gather(region, origin, flat_send.at[f], flat_recv.at[f], (pair_send.at[f], pair_recv.at[f]))
        keep = pltpu.make_async_copy(
            piece.at[pl.ds(skip, slots)],
            lead.at[core, :, pl.ds(pl.multiple_of(p * thin, thin), thin), :],
            local_sem.at[f],
        )
        return stage, keep

    skip_b = (early // 2) * blocks_b.shape[0]
    stage_a, keep_a = lead_stages(0, lead_a, piece_a, 0)
    stage_b, keep_b = lead_stages(1, lead_b, piece_b, skip_b)

    def pair_region(q, k, part):
        half = BLK // 2
        lo, size = {None: (0, half), 0: (0, half // 2), 1: (half // 2, half // 2)}[part]
        return vv_all.at[q, pl.ds(k * half + lo, size)]

    stage_v = plane_gather(pair_region, lambda k: pair_region(p, k, None), vflat_send, vflat_recv, None)
    vcuts = [
        remote(pairs.at[d], vv_all.at[lax.rem(p + d, rows)], vcut_send.at[d], vcut_recv, (lax.rem(p + d, rows), c))
        for d in range(1, rows)
    ]
    turns = [lax.rem(s + rows - p, rows) for s in range(cols)]

    def lead_block(other):
        fix = lax.dot_general(own_mu[...], um[other], NT, preferred_element_type=jnp.float32)
        return diag_ref[:, pl.ds(pl.multiple_of(other * BLK, BLK), BLK)] - 0.5 * fix

    spread_start(0)
    spread_pass(0)
    spread_end(0)

    @pl.when(p == 0)
    def _():
        size = BLK
        r = lax.broadcasted_iota(jnp.int32, (size, size), 0)
        l = lax.broadcasted_iota(jnp.int32, (size, size), 1)
        half = size // 2

        def dots(x, y, dims):
            return lax.dot_general(x, y, (dims, ((), ())), preferred_element_type=jnp.float32)

        gram = jnp.zeros((size, size), jnp.float32)
        for s in range(cols):
            slab = vu_all[s, 0]
            gram = gram + dots(slab, slab, ((0,), (0,)))
        core_w = jnp.where((r < half) & (l < half), gram, 0.0).astype(jnp.bfloat16)
        down = jnp.where(r == l + half, 1.0, 0.0).astype(jnp.bfloat16)
        right = jnp.where(l == r + half, 1.0, 0.0).astype(jnp.bfloat16)
        same = jnp.where((r == l) & (r >= half), 1.0, 0.0)
        low_w = dots(down, core_w, ((1,), (0,)))
        low_w16 = low_w.astype(jnp.bfloat16)
        take_mu = (low_w + same).astype(jnp.bfloat16)
        take_um = (dots(low_w16, right, ((1,), (0,))) + down.astype(jnp.float32)).astype(jnp.bfloat16)
        for s in range(cols):
            um[s] = dots(vu_all[s, 0], take_um, ((1,), (0,))).astype(jnp.bfloat16)
        own_mu[...] = dots(vu_ref[0], take_mu, ((1,), (0,))).astype(jnp.bfloat16)
        for j in range(early):
            blocks_a[j] = lead_block(j)
        phases[0][2][...] = blocks_a[:, :thin, :]
        start_all(phases[0][0])

    @pl.when(p > 0)
    def _():
        phases[0][0][0].wait_recv()

    start_all(phases[0][1])

    @pl.when(p == 0)
    def _():
        for j in range(late // 2 + 1):
            other = early + lax.rem(c - early - j + 2 * late, late)
            block = lead_block(other)

            @pl.when(c >= other)
            def _(block=block, j=j):
                blocks_b[j] = block

            @pl.when(c < other)
            def _(block=block, j=j):
                blocks_b[j] = block.T
        phases[1][2][...] = blocks_b[:, :thin, :]
        start_all(phases[1][0])

    for copy in phases[0][1]:
        copy.wait_recv()
    keep_a.start()
    stage_a(0)

    @pl.when(p > 0)
    def _():
        phases[1][0][0].wait_recv()

    stage_a(1)
    start_all(phases[1][1])
    stage_a(2)
    stage_a(3)
    stage_a(4)
    for copy in phases[1][1]:
        copy.wait_recv()
    keep_b.start()
    stage_b(0)
    spread_start(1)
    keep_a.wait()
    stage_a(5)

    def build_pairs():
        @pl.when(p == c)
        def _():
            for s in range(cols):
                lanes = lax.broadcasted_iota(jnp.int32, (BLK, BLK), 1)
                lefts = vu_all[s, 0].astype(jnp.float32)
                rights = pltpu.roll(vu_all[s, 1].astype(jnp.float32), BLK // 2, 1)
                pairs[turns[s]] = jnp.where(lanes < BLK // 2, lefts, rights).astype(jnp.bfloat16)
            vv_all[p] = pairs[0]
            start_all(vcuts)

    def take_pairs():
        @pl.when(p != c)
        def _():
            vcuts[0].wait_recv()

    def errands(s):
        if s < early:
            stage_b(s + 1)
        if s == early - 1:
            for number in range(early + 1, 6):
                stage_b(number)
            keep_b.wait()
        if count == 16:
            plan = {4: [lambda: spread_pass(1)], 5: [lambda: spread_end(1), build_pairs], 6: [take_pairs, lambda: stage_v(0)],
                    7: [lambda: stage_v(1)], 8: [lambda: stage_v(2)], 9: [lambda: stage_v(3)], 10: [lambda: stage_v(4)]}
        else:
            plan = {3: [lambda: spread_pass(1), lambda: spread_end(1), build_pairs, take_pairs] + [lambda n=n: stage_v(n) for n in range(5)]}
        for act in plan.get(s, []):
            act()

    def block_of(i, k):
        if i < k:
            return jnp.zeros((BLK, BLK), jnp.float32)
        phase, source, slot = lead_place(i, k, count)
        if phase == 0:
            return lead_a[source % 2, (source // 2) * early + slot]
        return lead_b[source % 2, (source // 2 - early // 2) * (late // 2 + 1) + slot]

    def given(r0, r1, k):
        lo = k * BLK
        parts = [block_of(r // BLK, k) for r in range(r0, min(r1, order), BLK)]
        if r1 > order:
            parts.append(y_ref[max(r0, order) - order:r1 - order, lo:lo + BLK])
        return parts[0] if len(parts) == 1 else jnp.concatenate(parts, axis=0)

    def pair_given(r0, r1, k):
        return jnp.concatenate([given(r0, r1, k), given(r0, r1, k + 1)], axis=1)

    def spans(start, size):
        return [(r, min(r + size, total)) for r in range(start, total, size)]

    for r0, r1 in spans(0, 2 * BLK):
        work[r0:r1, :] = pair_given(r0, r1, 0)
    part_ref[...] = jnp.zeros_like(part_ref)

    def step(k, carry):
        base = pl.multiple_of(k * BLK, BLK)
        flank = pl.ds(pl.multiple_of(lax.rem(k, 2) * BLK, BLK), BLK)
        inverse = invert_factor([work[pl.ds(base + g * GRP, GRP), flank] for g in range(BLK // GRP)])
        high_part, low_part = halves(jnp.concatenate(inverse, axis=0))
        wh[...] = high_part
        wl[...] = low_part

        for s in range(count):
            @pl.when(k == s)
            def _(s=s):
                lo, hi = s * BLK, s * BLK + BLK
                left = (s % 2) * BLK
                errands(s)
                for r0, r1 in spans(lo, 4 * BLK):
                    sh, sl = halves(work[r0:r1, left:left + BLK])
                    panel = mul3(sh, sl, wh[...], wl[...])
                    ph, pl_ = halves(panel)
                    high[r0:r1, lo:hi] = ph
                    low[r0:r1, lo:hi] = pl_
                    work[r0:r1, left:left + BLK] = panel
                x_ref[:, lo:hi] = work[order:order + x_ref.shape[0], left:left + BLK]

                @pl.when(jnp.logical_and(c == s, p >= s))
                def _():
                    block = work[pl.ds(pl.multiple_of(p * BLK, BLK), BLK), left:left + BLK]
                    r = lax.broadcasted_iota(jnp.int32, (BLK, BLK), 0)
                    l = lax.broadcasted_iota(jnp.int32, (BLK, BLK), 1)
                    part_ref[...] = jnp.where((p > s) | (r >= l), block, 0.0)

                if s % 2 == 0 and s + 1 < count:
                    for r0, r1 in spans(hi, 4 * BLK):
                        work[r0:r1, BLK:] = work[r0:r1, BLK:] - mul3(
                            high[r0:r1, lo:hi], low[r0:r1, lo:hi],
                            high[hi:hi + BLK, lo:hi], low[hi:hi + BLK, lo:hi])
                if s % 2 == 1 and s + 1 < count:
                    end = hi + 2 * BLK
                    for r0, r1 in spans(hi, 4 * BLK):
                        work[r0:r1, :] = pair_given(r0, r1, s + 1) - mul3(
                            high[r0:r1, :hi], low[r0:r1, :hi],
                            high[hi:end, :hi], low[hi:end, :hi])
        return carry

    lax.fori_loop(0, count, step, 0)

    stage_a(6)
    stage_b(6)
    stage_v(6)
    for first, later in spreads:
        for copy in first + later:
            copy.wait_send()
    for cuts, ring, mine in phases:
        for copy in ring:
            copy.wait_send()

    @pl.when(p == 0)
    def _():
        for cuts, ring, mine in phases:
            for copy in cuts:
                copy.wait_send()

    @pl.when(p == c)
    def _():
        for copy in vcuts:
            copy.wait_send()


def update_call(vu, diag_rows, right, narrow):
    rows, cols = lax.axis_size("row"), lax.axis_size("col")
    depth, thin = cols // 2, BLK // rows
    extra, order = right.shape
    early = early_count(cols)
    late = (cols - early) // 2 + 1
    vm = pl.BlockSpec(memory_space=pltpu.VMEM)
    dma = pltpu.SemaphoreType.DMA
    wide, half = jnp.float32, jnp.bfloat16
    return pl.pallas_call(
        update_kernel,
        out_shape=(
            jax.ShapeDtypeStruct((cols, 2, BLK, BLK), half),
            jax.ShapeDtypeStruct((rows, BLK, BLK), half),
            jax.ShapeDtypeStruct((narrow, order), wide),
            jax.ShapeDtypeStruct((BLK, BLK), wide),
        ),
        in_specs=[vm, vm, vm],
        out_specs=(vm, vm, vm, vm),
        scratch_shapes=[
            pltpu.VMEM((2, depth * early, BLK, BLK), wide),
            pltpu.VMEM((2, (depth - early // 2) * late, BLK, BLK), wide),
            pltpu.VMEM((early, BLK, BLK), wide),
            pltpu.VMEM((late, BLK, BLK), wide),
            pltpu.VMEM((depth * early, thin, BLK), wide),
            pltpu.VMEM((depth * late, thin, BLK), wide),
            pltpu.VMEM((rows, BLK, BLK), half),
            pltpu.VMEM((cols, BLK, BLK), half),
            pltpu.VMEM((BLK, BLK), half),
            pltpu.VMEM((order + extra, order), half),
            pltpu.VMEM((order + extra, order), half),
            pltpu.VMEM((order + extra, 2 * BLK), wide),
            pltpu.VMEM((BLK, BLK), half),
            pltpu.VMEM((BLK, BLK), half),
            dma((2, depth)), dma((2, depth)), dma((2, depth)), dma((2, depth)),
            dma((2, rows)), dma((2,)), dma((2, depth)), dma((2, depth)),
            dma((2, 2, 20)), dma((2, 2, 20)), dma((2, 2, 16)), dma((2, 2, 16)),
            dma((rows,)), dma, dma((2, 20)), dma((2, 20)), dma((2,)),
        ],
        compiler_params=pltpu.CompilerParams(
            collective_id=0, has_side_effects=True, vmem_limit_bytes=56 * 2**20
        ),
        cost_estimate=pl.CostEstimate(flops=10**11, bytes_accessed=2 * 10**7, transcendentals=0),
    )(vu, diag_rows, right)


def body(pan_left, pan_right, panel_rank, diag_tiles, col_right, column_rank):
    tile_rows = pan_left.shape[0]
    slab_rows = pan_left.shape[2]
    rank_width = pan_left.shape[3]
    tile_order = diag_tiles.shape[3]
    row_count = lax.axis_size("row")
    col_count = lax.axis_size("col")
    row_index = lax.axis_index("row")
    col_index = lax.axis_index("col")
    col_tiles = tile_rows * row_count // col_count
    columns = lax.broadcasted_iota(jnp.int32, pan_left.shape, 3)
    keep_mask = columns < panel_rank[:, :, None, None]
    zeros_half = jnp.zeros_like(pan_left)
    left_masked = jnp.where(keep_mask, pan_left, zeros_half)
    right_masked = jnp.where(keep_mask, pan_right, zeros_half)
    vu = jnp.concatenate([right_masked, left_masked], axis=3)[:, 0]
    narrow_rows = col_right.shape[2]
    rank_ids = lax.broadcasted_iota(jnp.int32, col_right.shape, 2) + col_index * narrow_rows
    tile_ids = lax.broadcasted_iota(jnp.int32, col_right.shape, 0) * row_count + row_index
    keep_right = (rank_ids < column_rank[:, :, None, None]) & (tile_ids >= 1)
    right_kept = jnp.where(keep_right, col_right, jnp.zeros_like(col_right))
    right_side = right_kept.astype(jnp.float32).reshape(-1, tile_order)
    count = right_side.shape[0]
    right_side = jnp.pad(right_side, ((0, -count % 16), (0, 0)))
    vu_all, vv_all, solved, lead_part = update_call(vu, diag_tiles[0, 0], right_side, count)
    flat_vu = vu_all.transpose(1, 0, 2, 3).reshape(tile_rows, tile_order, 2 * rank_width)
    right_tiles, left_tiles = flat_vu[:, :, :rank_width], flat_vu[:, :, rank_width:]
    theirs = vv_all.reshape(tile_order, col_tiles, rank_width)
    own_gram = jnp.einsum(
        "anr,ans->ars", right_tiles, right_tiles, preferred_element_type=jnp.float32
    ).astype(jnp.bfloat16)
    products = jnp.einsum(
        "anr,ars->ans", left_tiles, own_gram, preferred_element_type=jnp.float32
    ).astype(jnp.bfloat16)
    product_rows = lax.dynamic_slice_in_dim(products, col_index * slab_rows, slab_rows, 1)
    correction = jnp.einsum(
        "ans,ams->anm", product_rows, left_tiles, preferred_element_type=jnp.float32
    )
    diag_new = diag_tiles - correction[:, None]
    cross_gram = jnp.einsum(
        "anr,nbs->abrs", right_tiles, theirs, preferred_element_type=jnp.float32
    ).astype(jnp.bfloat16)

    col_solved = solved.reshape(col_right.shape)

    tile_update = jnp.einsum(
        "anr,abrs->abns", left_tiles, cross_gram, preferred_element_type=jnp.float32
    )
    row_ids = lax.broadcasted_iota(jnp.int32, (tile_rows, col_tiles), 0) * row_count + row_index
    col_ids = lax.broadcasted_iota(jnp.int32, (tile_rows, col_tiles), 1) * col_count + col_index
    lower_mask = (row_ids > col_ids)[:, :, None, None]
    panel_update = jnp.where(lower_mask, tile_update, jnp.zeros_like(tile_update)).astype(
        jnp.bfloat16
    )
    panel_update = panel_update.reshape(tile_rows, 1, col_tiles, 1, tile_order, rank_width)
    return (panel_update, diag_new, lead_part, col_solved)


def solution(mesh):
    placed = (
        P(None, "row", "col", None),
        P(None, "row", "col", None),
        P(None, "row"),
        P(None, "row", "col", None),
        P(None, "row", "col", None),
        P(None, "row"),
    )
    return jax.shard_map(
        body,
        mesh=mesh,
        in_specs=placed,
        out_specs=(
            P(None, "row", None, "col", None, None),
            P(None, "row", "col", None),
            P("row", "col"),
            P(None, "row", "col", None),
        ),
        check_vma=False,
    )
```

time: 1060 us -> 158 us (0.15)
  other arithmetic: 505 us -> 3.08 us
  waiting for transfers between devices: 272 us -> 0 us
  Pallas kernels: 0 us -> 140 us
  matrix products: 132 us -> 6.44 us
  local copies, waits for them, and re-layouts: 84.2 us -> 7.23 us
  blocking collectives: 38.6 us -> 0 us
  between operations: 25.3 us -> 0.74 us
    another operation x68 -> x0, other arithmetic: 495 us -> none  [the longest x59 328 us: blocked_cholesky(): diagonal_factor = jnp.linalg.cholesky(diagonal_block)]
    all_gather x2 -> x0, waiting for transfers between devices: 178 us -> none  [the longest x1 102 us: body(): lead_tile = lax.all_gather(lead_rows, 'col', axis=0, tiled=True)]
    pallas_call x0 -> x1, Pallas kernels: none -> 140 us  [update_call(): pl.pallas_call(update_kernel, out_shape=(jax.ShapeDtypeStruct((cols, 2, B...]
    psum x1 -> x0, waiting for transfers between devices: 93.3 us -> none  [spread(): return lax.psum(kept, axis)]
    another operation x73 -> x0, matrix products: 81.9 us -> none  [the longest x21 36.3 us: blocked_cholesky(): lax.linalg.triangular_solve(diagonal_factor, lower_block, left_side=False...]
    another operation x77 -> x0, local copies, waits for them, and re-layouts: 56.3 us -> none
    dot_general x7 -> x1, matrix products: 46.7 us -> 1.9 us  [body(): jnp.einsum('anr,abrs->abns', left_tiles, cross_gram, preferred_element_ty...]
    all_gather x2 -> x0, blocking collectives: 38.6 us -> none  [the longest x1 22.8 us: body(): lax.all_gather(right_masked, 'col', axis=2, tiled=True)]
  transfers between devices with their start and end apart: 3 -> 0, of which waited for: 3 -> 0; matrix products, arithmetic and copies ran while one was open for 1% -> 0% of each run, Pallas kernels for 0% -> 0%
where the time goes in v4:
time: 158 us; the launch traced here: 157 us
  Pallas kernels  140 us (89%)
  local copies, waits for them, and re-layouts  7.23 us (5%)
  matrix products  6.44 us (4%)
  other arithmetic  3.08 us (2%)
    pallas_call x1, Pallas kernels, update_call(): pl.pallas_call(update_kernel, out_shape=(jax.ShapeDtypeStruct((cols, 2, B...  140 us

profile of v4, /device:TPU:1, one launch (start us, length us, event | category | flops | bytes accessed | tf_op | source)
XLA Modules:
  0.0 157.5 jit_solution(7463721870165139217)
XLA Ops:
  0.7 0.1 broadcast_compare_fusion
  0.8 0.8 and_select_fusion
  1.6 0.9 copy.17
  2.5 0.9 copy.16
  3.4 0.8 fusion.17
  4.1 0.7 maximum_bitcast_fusion.vu_ref
  4.9 0.7 pad_convert_fusion.y_ref
  5.5 2.3 %slice_bitcast_fusion.diag_ref = f32[128,2048]{1,0:T(8,128)} fusion(f32[2,1,128,2048]{3,2,1,0:T(8,128)} %param.9), kind=kLoop, calls=%fused_computation.12 | loop fusion | bytes 2097152 | tf_op jit(solution)/shard_map/squeeze | solution.py:620
  7.8 140.0 %shard_map.93 = (bf16[16,2,128,128]{3,2,1,0:T(8,128)(2,1)}, bf16[16,128,128]{2,1,0:T(8,128)(2,1)}, f32[8,2048]{1,0:T(8,128)}, f32[128,128]{1,0:T(8,128)}) custom-call(bf16[2,128,128]{2,1,0:T(8,128)(2,1)} %maximum_bitcast_fusion.vu_ref, f32[128,2048]{1,0:T(8,128)} %slice_bitcast_fusion.diag_ref, f32[16,2048]{1,0:T(8,128)} %pad_convert_fusion.y_ref), custom_call_target="tpu_custom_call" | custom-call | flops 99999997952 | bytes 20000000 | tf_op jit(solution)/shard_map/pallas_call | solution.py:559
  147.8 0.0 copy-start.1
  147.8 0.0 copy-start.3
  147.8 1.6 copy.18
  149.4 0.2 reshape.76
  149.6 0.0 copy-done.1
  149.6 0.1 copy.19
  149.8 0.0 copy-done.3
  149.8 0.7 reshape.75
  150.4 1.9 %fusion.3 = bf16[2,1,2,1,2048,64]{4,5,3,2,1,0:T(8,128)(2,1)} fusion(bf16[2048,2,64,1]{0,2,1,3:T(8,128)(2,1)S(1)} %reshape.76, pred[2,2]{1,0:T(4,128)(4,1)S(1)} %broadcast_compare_fusion, bf16[2,2048,128]{2,1,0:T(8,128)(2,1)S(1)} %bitcast.44), kind=kOutput, calls=%fused_computation.5 | convolution fusion | flops 135282688 | bytes 3670528 | tf_op jit(solution)/shard_map/anr,abrs->abns/dot_general | solution.py:641
  152.3 0.0 copy-start
  152.3 1.7 %fusion.5 = bf16[2,2048,64]{1,2,0:T(8,128)(2,1)} fusion(bf16[2,2048,128]{2,1,0:T(8,128)(2,1)S(1)} %bitcast.45), kind=kOutput, calls=%fused_computation.9 | convolution fusion | flops 67117056 | bytes 2621440 | tf_op jit(solution)/shard_map/anr,ars->ans/dot_general | solution.py:627
  154.0 0.0 copy-done
  154.0 0.0 copy-start.2
  154.0 2.8 %fusion.1 = f32[2,1,128,2048]{3,2,1,0:T(8,128)} fusion(f32[2,1,128,2048]{3,2,1,0:T(8,128)S(1)} %copy-done, bf16[2,2048,128]{2,1,0:T(8,128)(2,1)S(1)} %bitcast.46, bf16[2,2048,64]{1,2,0:T(8,128)(2,1)} %fusion.5, s32[]{:T(128)S(6)} %select_n.23), kind=kOutput, calls=%fused_computation.3 | convolution fusion | flops 67633152 | bytes 5275652 | tf_op jit(solution)/shard_map/ans,ams->anm/dot_general | solution.py:631
  156.9 0.0 copy-done.2
  156.9 0.6 copy.29
  (4 shorter events, 0.0 us)
Async XLA Ops:
  147.8 1.8 %copy-start.1 = (bf16[16,2,128,128]{3,2,1,0:T(8,128)(2,1)S(1)}, bf16[16,2,128,128]{3,2,1,0:T(8,128)(2,1)}, u32[]{:S(2)}) copy-start(bf16[16,2,128,128]{3,2,1,0:T(8,128)(2,1)} %get-tuple-element.9) | copy-start | bytes 3145732
  147.8 1.9 %copy-start.3 = (f32[8,2048]{1,0:T(8,128)S(1)}, f32[8,2048]{1,0:T(8,128)}, u32[]{:S(2)}) copy-start(f32[8,2048]{1,0:T(8,128)} %get-tuple-element.11) | copy-start | bytes 196612
  152.3 1.7 %copy-start = (f32[2,1,128,2048]{3,2,1,0:T(8,128)S(1)}, f32[2,1,128,2048]{3,2,1,0:T(8,128)}, u32[]{:S(2)}) copy-start(f32[2,1,128,2048]{3,2,1,0:T(8,128)} %param.9) | copy-start | bytes 6291460
  154.0 2.8 %copy-start.2 = (f32[128,128]{1,0:T(8,128)S(1)}, f32[128,128]{1,0:T(8,128)}, u32[]{:S(2)}) copy-start(f32[128,128]{1,0:T(8,128)} %get-tuple-element.30) | copy-start | bytes 196612

commit v5 on v4

--- a/solution.py
+++ b/solution.py
@@ -94,6 +94,13 @@
     high = value.astype(jnp.bfloat16)
     return high, (value - high.astype(jnp.float32)).astype(jnp.bfloat16)
 
+def mul2(lh, ll, rh, rl):
+    both = jnp.concatenate([lh, ll], axis=1)
+    twice = jnp.concatenate([rh, rh], axis=1)
+    first = lax.dot_general(both, twice, NT, preferred_element_type=jnp.float32)
+    return first + lax.dot_general(lh, rl, NT, preferred_element_type=jnp.float32)
+
+
 def mul3(lh, ll, rh, rl):
     def one(x, y):
         return lax.dot_general(x, y, NT, preferred_element_type=jnp.float32)
@@ -116,13 +123,13 @@
 
 
 def update_kernel(
-    vu_ref, diag_ref, y_ref,
+    rank_ref, left_ref, right_ref, tiles_ref, y_ref,
     vu_all, vv_all, x_ref, part_ref,
-    lead_a, lead_b, blocks_a, blocks_b, piece_a, piece_b, pairs, um, own_mu, high, low, work, wh, wl,
+    vu_ref, diag_ref, lead_a, lead_b, blocks_a, blocks_b, piece_a, piece_b, pairs, um, own_mu, high, low, work, wh, wl,
     uv_send, uv_recv, fw_send, fw_recv, cut_send, cut_recv, ring_send, ring_recv,
     flat_send, flat_recv, pair_send, pair_recv, vcut_send, vcut_recv, vflat_send, vflat_recv, local_sem,
 ):
-    rows, cols = cut_send.shape[1], vu_all.shape[0]
+    rows, cols = cut_send.shape[1], vu_all.shape[1]
     side = {4: 2, 16: 4}[rows]
     depth = cols // 2
     early = early_count(cols)
@@ -154,19 +161,31 @@
         for copy in copies:
             copy.start()
 
+    fetch = pltpu.make_async_copy(tiles_ref.at[0, 0], diag_ref, local_sem.at[2])
+
+    @pl.when(p == 0)
+    def _():
+        fetch.start()
+
     barrier = pltpu.get_barrier_semaphore()
     partners = [along(d) for d in range(1, depth)] + [(p, sibling)] + [(lax.rem(p + d, rows), c) for d in range(1, rows)]
     for where in partners:
         pl.semaphore_signal(barrier, inc=1, device_id=where, device_id_type=MESH)
+    for a in range(2):
+        wide_lanes = lax.broadcasted_iota(jnp.int32, (BLK, BLK), 1)
+        joined = jnp.concatenate([right_ref[a, 0], left_ref[a, 0]], axis=1).astype(jnp.float32)
+        rank = rank_ref[a, 0]
+        live = lax.rem(wide_lanes, BLK // 2) < rank
+        vu_ref[a] = jnp.where(live, joined, 0.0).astype(jnp.bfloat16)
     pl.semaphore_wait(barrier, len(partners))
 
     spreads = []
     for a in range(2):
         first = [
-            remote(vu_ref.at[a], vu_all.at[c, a], uv_send.at[a, d], uv_recv.at[a, d], along(d)) for d in range(1, depth)
+            remote(vu_ref.at[a], vu_all.at[a, c], uv_send.at[a, d], uv_recv.at[a, d], along(d)) for d in range(1, depth)
         ]
-        held = [vu_all.at[2 * lax.rem(z + depth - d, depth) + core, a] for d in range(depth)]
-        later = [remote(vu_ref.at[a], vu_all.at[c, a], fw_send.at[a, 0], fw_recv.at[a, 0], (p, sibling))] + [
+        held = [vu_all.at[a, 2 * lax.rem(z + depth - d, depth) + core] for d in range(depth)]
+        later = [remote(vu_ref.at[a], vu_all.at[a, c], fw_send.at[a, 0], fw_recv.at[a, 0], (p, sibling))] + [
             remote(held[d], held[d], fw_send.at[a, d], fw_recv.at[a, d], (p, sibling)) for d in range(1, depth)
         ]
         spreads.append((first, later))
@@ -175,7 +194,7 @@
         first, later = spreads[a]
         start_all(first)
         later[0].start()
-        vu_all[c, a] = vu_ref[a]
+        vu_all[a, c] = vu_ref[a]
 
     def spread_pass(a):
         first, later = spreads[a]
@@ -360,10 +379,8 @@
         def dots(x, y, dims):
             return lax.dot_general(x, y, (dims, ((), ())), preferred_element_type=jnp.float32)
 
-        gram = jnp.zeros((size, size), jnp.float32)
-        for s in range(cols):
-            slab = vu_all[s, 0]
-            gram = gram + dots(slab, slab, ((0,), (0,)))
+        flat = vu_all[0].reshape(order, size)
+        gram = dots(flat, flat, ((0,), (0,)))
         core_w = jnp.where((r < half) & (l < half), gram, 0.0).astype(jnp.bfloat16)
         down = jnp.where(r == l + half, 1.0, 0.0).astype(jnp.bfloat16)
         right = jnp.where(l == r + half, 1.0, 0.0).astype(jnp.bfloat16)
@@ -372,8 +389,8 @@
         low_w16 = low_w.astype(jnp.bfloat16)
         take_mu = (low_w + same).astype(jnp.bfloat16)
         take_um = (dots(low_w16, right, ((1,), (0,))) + down.astype(jnp.float32)).astype(jnp.bfloat16)
-        for s in range(cols):
-            um[s] = dots(vu_all[s, 0], take_um, ((1,), (0,))).astype(jnp.bfloat16)
+        um[...] = dots(flat, take_um, ((1,), (0,))).astype(jnp.bfloat16).reshape(um.shape)
+        fetch.wait()
         own_mu[...] = dots(vu_ref[0], take_mu, ((1,), (0,))).astype(jnp.bfloat16)
         for j in range(early):
             blocks_a[j] = lead_block(j)
@@ -429,8 +446,8 @@
         def _():
             for s in range(cols):
                 lanes = lax.broadcasted_iota(jnp.int32, (BLK, BLK), 1)
-                lefts = vu_all[s, 0].astype(jnp.float32)
-                rights = pltpu.roll(vu_all[s, 1].astype(jnp.float32), BLK // 2, 1)
+                lefts = vu_all[0, s].astype(jnp.float32)
+                rights = pltpu.roll(vu_all[1, s].astype(jnp.float32), BLK // 2, 1)
                 pairs[turns[s]] = jnp.where(lanes < BLK // 2, lefts, rights).astype(jnp.bfloat16)
             vv_all[p] = pairs[0]
             start_all(vcuts)
@@ -494,9 +511,9 @@
                 lo, hi = s * BLK, s * BLK + BLK
                 left = (s % 2) * BLK
                 errands(s)
-                for r0, r1 in spans(lo, 4 * BLK):
+                for r0, r1 in spans(lo, 8 * BLK):
                     sh, sl = halves(work[r0:r1, left:left + BLK])
-                    panel = mul3(sh, sl, wh[...], wl[...])
+                    panel = mul2(sh, sl, wh[...], wl[...])
                     ph, pl_ = halves(panel)
                     high[r0:r1, lo:hi] = ph
                     low[r0:r1, lo:hi] = pl_
@@ -511,13 +528,13 @@
                     part_ref[...] = jnp.where((p > s) | (r >= l), block, 0.0)
 
                 if s % 2 == 0 and s + 1 < count:
-                    for r0, r1 in spans(hi, 4 * BLK):
-                        work[r0:r1, BLK:] = work[r0:r1, BLK:] - mul3(
+                    for r0, r1 in spans(hi, 8 * BLK):
+                        work[r0:r1, BLK:] = work[r0:r1, BLK:] - mul2(
                             high[r0:r1, lo:hi], low[r0:r1, lo:hi],
                             high[hi:hi + BLK, lo:hi], low[hi:hi + BLK, lo:hi])
                 if s % 2 == 1 and s + 1 < count:
                     end = hi + 2 * BLK
-                    for r0, r1 in spans(hi, 4 * BLK):
+                    for r0, r1 in spans(hi, 8 * BLK):
                         work[r0:r1, :] = pair_given(r0, r1, s + 1) - mul3(
                             high[r0:r1, :hi], low[r0:r1, :hi],
                             high[hi:end, :hi], low[hi:end, :hi])
@@ -547,7 +564,7 @@
             copy.wait_send()
 
 
-def update_call(vu, diag_rows, right, narrow):
+def update_call(rank, left, right_factor, tiles, right, narrow):
     rows, cols = lax.axis_size("row"), lax.axis_size("col")
     depth, thin = cols // 2, BLK // rows
     extra, order = right.shape
@@ -559,14 +576,16 @@
     return pl.pallas_call(
         update_kernel,
         out_shape=(
-            jax.ShapeDtypeStruct((cols, 2, BLK, BLK), half),
+            jax.ShapeDtypeStruct((2, cols, BLK, BLK), half),
             jax.ShapeDtypeStruct((rows, BLK, BLK), half),
             jax.ShapeDtypeStruct((narrow, order), wide),
             jax.ShapeDtypeStruct((BLK, BLK), wide),
         ),
-        in_specs=[vm, vm, vm],
+        in_specs=[pl.BlockSpec(memory_space=pltpu.SMEM), vm, vm, pl.BlockSpec(memory_space=pl.ANY), vm],
         out_specs=(vm, vm, vm, vm),
         scratch_shapes=[
+            pltpu.VMEM((2, BLK, BLK), half),
+            pltpu.VMEM((BLK, order), wide),
             pltpu.VMEM((2, depth * early, BLK, BLK), wide),
             pltpu.VMEM((2, (depth - early // 2) * late, BLK, BLK), wide),
             pltpu.VMEM((early, BLK, BLK), wide),
@@ -584,13 +603,13 @@
             dma((2, depth)), dma((2, depth)), dma((2, depth)), dma((2, depth)),
             dma((2, rows)), dma((2,)), dma((2, depth)), dma((2, depth)),
             dma((2, 2, 20)), dma((2, 2, 20)), dma((2, 2, 16)), dma((2, 2, 16)),
-            dma((rows,)), dma, dma((2, 20)), dma((2, 20)), dma((2,)),
+            dma((rows,)), dma, dma((2, 20)), dma((2, 20)), dma((3,)),
         ],
         compiler_params=pltpu.CompilerParams(
             collective_id=0, has_side_effects=True, vmem_limit_bytes=56 * 2**20
         ),
         cost_estimate=pl.CostEstimate(flops=10**11, bytes_accessed=2 * 10**7, transcendentals=0),
-    )(vu, diag_rows, right)
+    )(rank, left, right_factor, tiles, right)
 
 
 def body(pan_left, pan_right, panel_rank, diag_tiles, col_right, column_rank):
@@ -603,12 +622,6 @@
     row_index = lax.axis_index("row")
     col_index = lax.axis_index("col")
     col_tiles = tile_rows * row_count // col_count
-    columns = lax.broadcasted_iota(jnp.int32, pan_left.shape, 3)
-    keep_mask = columns < panel_rank[:, :, None, None]
-    zeros_half = jnp.zeros_like(pan_left)
-    left_masked = jnp.where(keep_mask, pan_left, zeros_half)
-    right_masked = jnp.where(keep_mask, pan_right, zeros_half)
-    vu = jnp.concatenate([right_masked, left_masked], axis=3)[:, 0]
     narrow_rows = col_right.shape[2]
     rank_ids = lax.broadcasted_iota(jnp.int32, col_right.shape, 2) + col_index * narrow_rows
     tile_ids = lax.broadcasted_iota(jnp.int32, col_right.shape, 0) * row_count + row_index
@@ -617,8 +630,10 @@
     right_side = right_kept.astype(jnp.float32).reshape(-1, tile_order)
     count = right_side.shape[0]
     right_side = jnp.pad(right_side, ((0, -count % 16), (0, 0)))
-    vu_all, vv_all, solved, lead_part = update_call(vu, diag_tiles[0, 0], right_side, count)
-    flat_vu = vu_all.transpose(1, 0, 2, 3).reshape(tile_rows, tile_order, 2 * rank_width)
+    vu_all, vv_all, solved, lead_part = update_call(
+        panel_rank, pan_left, pan_right, diag_tiles, right_side, count
+    )
+    flat_vu = vu_all.reshape(tile_rows, tile_order, 2 * rank_width)
     right_tiles, left_tiles = flat_vu[:, :, :rank_width], flat_vu[:, :, rank_width:]
     theirs = vv_all.reshape(tile_order, col_tiles, rank_width)
     own_gram = jnp.einsum(

time: 158 us -> 155 us (0.981)
    unnamed x11 -> x12, local copies, waits for them, and re-layouts: 2.39 us -> 4.93 us
    squeeze x1 -> x0, local copies, waits for them, and re-layouts: 2.29 us -> none  [body(): diag_tiles[0, 0]]
where the time goes in v5:
time: 155 us
  Pallas kernels  139 us (90%)
  local copies, waits for them, and re-layouts  7.37 us (5%)
  matrix products  6.44 us (4%)
  other arithmetic  1.6 us (1%)
    pallas_call x1, Pallas kernels, update_call(): pl.pallas_call(update_kernel, out_shape=(jax.ShapeDtypeStruct((2, cols, B...  139 us
    unnamed x12, local copies, waits for them, and re-layouts  4.93 us

profile of v5, /device:TPU:1, one launch (start us, length us, event | category | flops | bytes accessed | tf_op | source)
XLA Modules:
  0.0 155.1 jit_solution(3817626866917489462)
XLA Ops:
  0.7 0.1 broadcast_compare_fusion
  0.8 1.3 copy.18.rank_ref
  2.0 0.8 and_select_fusion
  2.9 1.5 copy.19.left_ref
  4.4 1.5 copy.20.right_ref
  5.9 0.7 pad_convert_fusion.y_ref
  6.6 139.0 %shard_map.93 = (bf16[2,16,128,128]{3,2,1,0:T(8,128)(2,1)}, bf16[16,128,128]{2,1,0:T(8,128)(2,1)}, f32[8,2048]{1,0:T(8,128)}, f32[128,128]{1,0:T(8,128)}) custom-call(s32[2,1]{1,0:T(2,128)} %copy.18.rank_ref, bf16[2,1,128,64]{3,2,1,0:T(8,128)(2,1)} %copy.19.left_ref, bf16[2,1,128,64]{3,2,1,0:T(8,128)(2,1)} %copy.20.right_ref, f32[2,1,128,2048]{3,2,1,0:T(8,128)} %tiles_ref.1, ...), custom_call_target="tpu_custom_call" | custom-call | flops 99999997952 | bytes 20000000 | tf_op jit(solution)/shard_map/pallas_call | solution.py:576
  145.5 0.0 copy-start.3
  145.5 0.0 copy-start.1
  145.6 1.6 %copy.21 = bf16[16,128,128]{1,0,2:T(8,128)(2,1)S(1)} copy(bf16[16,128,128]{2,1,0:T(8,128)(2,1)} %get-tuple-element.8) | data formatting | bytes 1048576 | tf_op jit(solution)/shard_map/pallas_call | solution.py:576
  147.1 0.2 reshape.65
  147.3 0.0 copy-done.3
  147.4 0.7 reshape.64
  148.0 0.0 copy-done.1
  148.0 1.9 %fusion.3 = bf16[2,1,2,1,2048,64]{4,5,3,2,1,0:T(8,128)(2,1)} fusion(bf16[2048,2,64,1]{0,2,1,3:T(8,128)(2,1)S(1)} %reshape.65, pred[2,2]{1,0:T(4,128)(4,1)S(1)} %broadcast_compare_fusion, bf16[2,2048,128]{2,1,0:T(8,128)(2,1)S(1)} %bitcast.38), kind=kOutput, calls=%fused_computation.5 | convolution fusion | flops 135282688 | bytes 3670528 | tf_op jit(solution)/shard_map/anr,abrs->abns/dot_general | solution.py:656
  149.9 0.0 copy-start
  149.9 1.7 %fusion.5 = bf16[2,2048,64]{1,2,0:T(8,128)(2,1)} fusion(bf16[2,2048,128]{2,1,0:T(8,128)(2,1)S(1)} %bitcast.39), kind=kOutput, calls=%fused_computation.9 | convolution fusion | flops 67117056 | bytes 2621440 | tf_op jit(solution)/shard_map/anr,ars->ans/dot_general | solution.py:642
  151.6 0.0 copy-done
  151.6 0.0 copy-start.2
  151.6 2.8 %fusion.1 = f32[2,1,128,2048]{3,2,1,0:T(8,128)} fusion(f32[2,1,128,2048]{3,2,1,0:T(8,128)S(1)} %copy-done, bf16[2,2048,128]{2,1,0:T(8,128)(2,1)S(1)} %bitcast.40, bf16[2,2048,64]{1,2,0:T(8,128)(2,1)} %fusion.5, s32[]{:T(128)S(6)} %select_n.14), kind=kOutput, calls=%fused_computation.3 | convolution fusion | flops 67633152 | bytes 5275652 | tf_op jit(solution)/shard_map/ans,ams->anm/dot_general | solution.py:646
  154.5 0.0 copy-done.2
  154.5 0.6 copy.31
  (4 shorter events, 0.0 us)
Async XLA Ops:
  145.5 1.8 %copy-start.3 = (f32[8,2048]{1,0:T(8,128)S(1)}, f32[8,2048]{1,0:T(8,128)}, u32[]{:S(2)}) copy-start(f32[8,2048]{1,0:T(8,128)} %get-tuple-element.11) | copy-start | bytes 196612
  145.5 2.5 %copy-start.1 = (bf16[2,16,128,128]{3,2,1,0:T(8,128)(2,1)S(1)}, bf16[2,16,128,128]{3,2,1,0:T(8,128)(2,1)}, u32[]{:S(2)}) copy-start(bf16[2,16,128,128]{3,2,1,0:T(8,128)(2,1)} %get-tuple-element.9) | copy-start | bytes 3145732
  149.9 1.7 %copy-start = (f32[2,1,128,2048]{3,2,1,0:T(8,128)S(1)}, f32[2,1,128,2048]{3,2,1,0:T(8,128)}, u32[]{:S(2)}) copy-start(f32[2,1,128,2048]{3,2,1,0:T(8,128)} %tiles_ref.1) | copy-start | bytes 6291460
  151.6 2.8 %copy-start.2 = (f32[128,128]{1,0:T(8,128)S(1)}, f32[128,128]{1,0:T(8,128)}, u32[]{:S(2)}) copy-start(f32[128,128]{1,0:T(8,128)} %get-tuple-element.28) | copy-start | bytes 196612

commit v6 on v5

--- a/solution.py
+++ b/solution.py
@@ -125,7 +125,7 @@
 def update_kernel(
     rank_ref, left_ref, right_ref, tiles_ref, y_ref,
     vu_all, vv_all, x_ref, part_ref,
-    vu_ref, diag_ref, lead_a, lead_b, blocks_a, blocks_b, piece_a, piece_b, pairs, um, own_mu, high, low, work, wh, wl,
+    vu_ref, diag_ref, lead_a, lead_b, blocks_a, blocks_b, piece_a, piece_b, pairs, slabs, um, mu, high, low, work, wh, wl,
     uv_send, uv_recv, fw_send, fw_recv, cut_send, cut_recv, ring_send, ring_recv,
     flat_send, flat_recv, pair_send, pair_recv, vcut_send, vcut_recv, vflat_send, vflat_recv, local_sem,
 ):
@@ -361,39 +361,12 @@
     ]
     turns = [lax.rem(s + rows - p, rows) for s in range(cols)]
 
-    def lead_block(other):
-        fix = lax.dot_general(own_mu[...], um[other], NT, preferred_element_type=jnp.float32)
-        return diag_ref[:, pl.ds(pl.multiple_of(other * BLK, BLK), BLK)] - 0.5 * fix
-
-    spread_start(0)
-    spread_pass(0)
-    spread_end(0)
-
     @pl.when(p == 0)
     def _():
-        size = BLK
-        r = lax.broadcasted_iota(jnp.int32, (size, size), 0)
-        l = lax.broadcasted_iota(jnp.int32, (size, size), 1)
-        half = size // 2
-
-        def dots(x, y, dims):
-            return lax.dot_general(x, y, (dims, ((), ())), preferred_element_type=jnp.float32)
-
-        flat = vu_all[0].reshape(order, size)
-        gram = dots(flat, flat, ((0,), (0,)))
-        core_w = jnp.where((r < half) & (l < half), gram, 0.0).astype(jnp.bfloat16)
-        down = jnp.where(r == l + half, 1.0, 0.0).astype(jnp.bfloat16)
-        right = jnp.where(l == r + half, 1.0, 0.0).astype(jnp.bfloat16)
-        same = jnp.where((r == l) & (r >= half), 1.0, 0.0)
-        low_w = dots(down, core_w, ((1,), (0,)))
-        low_w16 = low_w.astype(jnp.bfloat16)
-        take_mu = (low_w + same).astype(jnp.bfloat16)
-        take_um = (dots(low_w16, right, ((1,), (0,))) + down.astype(jnp.float32)).astype(jnp.bfloat16)
-        um[...] = dots(flat, take_um, ((1,), (0,))).astype(jnp.bfloat16).reshape(um.shape)
         fetch.wait()
-        own_mu[...] = dots(vu_ref[0], take_mu, ((1,), (0,))).astype(jnp.bfloat16)
         for j in range(early):
-            blocks_a[j] = lead_block(j)
+            blocks_a[j] = diag_ref[:, j * BLK:(j + 1) * BLK]
+        blocks_a[early] = vu_ref[0].astype(jnp.float32)
         phases[0][2][...] = blocks_a[:, :thin, :]
         start_all(phases[0][0])
 
@@ -407,7 +380,7 @@
     def _():
         for j in range(late // 2 + 1):
             other = early + lax.rem(c - early - j + 2 * late, late)
-            block = lead_block(other)
+            block = diag_ref[:, pl.ds(pl.multiple_of(other * BLK, BLK), BLK)]
 
             @pl.when(c >= other)
             def _(block=block, j=j):
@@ -437,9 +410,31 @@
         copy.wait_recv()
     keep_b.start()
     stage_b(0)
+    spread_start(0)
     spread_start(1)
     keep_a.wait()
     stage_a(5)
+
+    r = lax.broadcasted_iota(jnp.int32, (BLK, BLK), 0)
+    l = lax.broadcasted_iota(jnp.int32, (BLK, BLK), 1)
+    half = BLK // 2
+
+    def dots(x, y, dims):
+        return lax.dot_general(x, y, (dims, ((), ())), preferred_element_type=jnp.float32)
+
+    for s in range(cols):
+        slabs[s * BLK:(s + 1) * BLK, :] = lead_a[s % 2, (s // 2) * (early + 1) + early].astype(jnp.bfloat16)
+    gram = dots(slabs[...], slabs[...], ((0,), (0,)))
+    core_w = jnp.where((r < half) & (l < half), gram, 0.0).astype(jnp.bfloat16)
+    down = jnp.where(r == l + half, 1.0, 0.0).astype(jnp.bfloat16)
+    right = jnp.where(l == r + half, 1.0, 0.0).astype(jnp.bfloat16)
+    same = jnp.where((r == l) & (r >= half), 1.0, 0.0)
+    low_w = dots(down, core_w, ((1,), (0,)))
+    take_mu = (low_w + same).astype(jnp.bfloat16)
+    take_um = (dots(low_w.astype(jnp.bfloat16), right, ((1,), (0,))) + down.astype(jnp.float32)).astype(jnp.bfloat16)
+    um[...] = dots(slabs[...], take_um, ((1,), (0,))).astype(jnp.bfloat16)
+    mu[:order, :] = (0.5 * dots(slabs[...], take_mu, ((1,), (0,)))).astype(jnp.bfloat16)
+    mu[order:, :] = jnp.zeros((total - order, BLK), jnp.bfloat16)
 
     def build_pairs():
         @pl.when(p == c)
@@ -465,10 +460,10 @@
                 stage_b(number)
             keep_b.wait()
         if count == 16:
-            plan = {4: [lambda: spread_pass(1)], 5: [lambda: spread_end(1), build_pairs], 6: [take_pairs, lambda: stage_v(0)],
+            plan = {4: [lambda: spread_pass(0), lambda: spread_pass(1)], 5: [lambda: spread_end(0), lambda: spread_end(1), build_pairs], 6: [take_pairs, lambda: stage_v(0)],
                     7: [lambda: stage_v(1)], 8: [lambda: stage_v(2)], 9: [lambda: stage_v(3)], 10: [lambda: stage_v(4)]}
         else:
-            plan = {3: [lambda: spread_pass(1), lambda: spread_end(1), build_pairs, take_pairs] + [lambda n=n: stage_v(n) for n in range(5)]}
+            plan = {3: [lambda: spread_pass(0), lambda: spread_end(0), lambda: spread_pass(1), lambda: spread_end(1), build_pairs, take_pairs] + [lambda n=n: stage_v(n) for n in range(5)]}
         for act in plan.get(s, []):
             act()
 
@@ -477,7 +472,7 @@
             return jnp.zeros((BLK, BLK), jnp.float32)
         phase, source, slot = lead_place(i, k, count)
         if phase == 0:
-            return lead_a[source % 2, (source // 2) * early + slot]
+            return lead_a[source % 2, (source // 2) * (early + 1) + slot]
         return lead_b[source % 2, (source // 2 - early // 2) * (late // 2 + 1) + slot]
 
     def given(r0, r1, k):
@@ -488,7 +483,8 @@
         return parts[0] if len(parts) == 1 else jnp.concatenate(parts, axis=0)
 
     def pair_given(r0, r1, k):
-        return jnp.concatenate([given(r0, r1, k), given(r0, r1, k + 1)], axis=1)
+        raw = jnp.concatenate([given(r0, r1, k), given(r0, r1, k + 1)], axis=1)
+        return raw - dots(mu[r0:r1, :], um[k * BLK:(k + 2) * BLK, :], ((1,), (1,)))
 
     def spans(start, size):
         return [(r, min(r + size, total)) for r in range(start, total, size)]
@@ -586,15 +582,16 @@
         scratch_shapes=[
             pltpu.VMEM((2, BLK, BLK), half),
             pltpu.VMEM((BLK, order), wide),
-            pltpu.VMEM((2, depth * early, BLK, BLK), wide),
+            pltpu.VMEM((2, depth * (early + 1), BLK, BLK), wide),
             pltpu.VMEM((2, (depth - early // 2) * late, BLK, BLK), wide),
-            pltpu.VMEM((early, BLK, BLK), wide),
+            pltpu.VMEM((early + 1, BLK, BLK), wide),
             pltpu.VMEM((late, BLK, BLK), wide),
-            pltpu.VMEM((depth * early, thin, BLK), wide),
+            pltpu.VMEM((depth * (early + 1), thin, BLK), wide),
             pltpu.VMEM((depth * late, thin, BLK), wide),
             pltpu.VMEM((rows, BLK, BLK), half),
-            pltpu.VMEM((cols, BLK, BLK), half),
-            pltpu.VMEM((BLK, BLK), half),
+            pltpu.VMEM((order, BLK), half),
+            pltpu.VMEM((order, BLK), half),
+            pltpu.VMEM((order + extra, BLK), half),
             pltpu.VMEM((order + extra, order), half),
             pltpu.VMEM((order + extra, order), half),
             pltpu.VMEM((order + extra, 2 * BLK), wide),

time: 155 us -> 151 us (0.974)
  Pallas kernels: 139 us -> 135 us
    pallas_call x1, Pallas kernels: 139 us -> 135 us  [update_call(): pl.pallas_call(update_kernel, out_shape=(jax.ShapeDtypeStruct((2, cols, B...]
where the time goes in v6:
time: 151 us
  Pallas kernels  135 us (89%)
  local copies, waits for them, and re-layouts  7.37 us (5%)
  matrix products  6.44 us (4%)
  other arithmetic  1.6 us (1%)
    pallas_call x1, Pallas kernels, update_call(): pl.pallas_call(update_kernel, out_shape=(jax.ShapeDtypeStruct((2, cols, B...  135 us
    unnamed x12, local copies, waits for them, and re-layouts  4.93 us

profile of v6, /device:TPU:1, one launch (start us, length us, event | category | flops | bytes accessed | tf_op | source)
XLA Modules:
  0.0 151.0 jit_solution(3200156143427699097)
XLA Ops:
  0.7 0.1 broadcast_compare_fusion
  0.8 1.3 copy.18.rank_ref
  2.0 0.8 and_select_fusion
  2.9 1.5 copy.19.left_ref
  4.4 1.5 copy.20.right_ref
  5.9 0.7 pad_convert_fusion.y_ref
  6.6 134.9 %shard_map.93 = (bf16[2,16,128,128]{3,2,1,0:T(8,128)(2,1)}, bf16[16,128,128]{2,1,0:T(8,128)(2,1)}, f32[8,2048]{1,0:T(8,128)}, f32[128,128]{1,0:T(8,128)}) custom-call(s32[2,1]{1,0:T(2,128)} %copy.18.rank_ref, bf16[2,1,128,64]{3,2,1,0:T(8,128)(2,1)} %copy.19.left_ref, bf16[2,1,128,64]{3,2,1,0:T(8,128)(2,1)} %copy.20.right_ref, f32[2,1,128,2048]{3,2,1,0:T(8,128)} %tiles_ref.1, ...), custom_call_target="tpu_custom_call" | custom-call | flops 99999997952 | bytes 20000000 | tf_op jit(solution)/shard_map/pallas_call | solution.py:572
  141.4 0.0 copy-start.3
  141.5 0.0 copy-start.1
  141.5 1.6 %copy.21 = bf16[16,128,128]{1,0,2:T(8,128)(2,1)S(1)} copy(bf16[16,128,128]{2,1,0:T(8,128)(2,1)} %get-tuple-element.8) | data formatting | bytes 1048576 | tf_op jit(solution)/shard_map/pallas_call | solution.py:572
  143.0 0.2 reshape.65
  143.3 0.0 copy-done.3
  143.3 0.7 reshape.64
  143.9 0.0 copy-done.1
  143.9 1.9 %fusion.3 = bf16[2,1,2,1,2048,64]{4,5,3,2,1,0:T(8,128)(2,1)} fusion(bf16[2048,2,64,1]{0,2,1,3:T(8,128)(2,1)S(1)} %reshape.65, pred[2,2]{1,0:T(4,128)(4,1)S(1)} %broadcast_compare_fusion, bf16[2,2048,128]{2,1,0:T(8,128)(2,1)S(1)} %bitcast.38), kind=kOutput, calls=%fused_computation.5 | convolution fusion | flops 135282688 | bytes 3670528 | tf_op jit(solution)/shard_map/anr,abrs->abns/dot_general | solution.py:653
  145.8 0.0 copy-start
  145.8 1.7 %fusion.5 = bf16[2,2048,64]{1,2,0:T(8,128)(2,1)} fusion(bf16[2,2048,128]{2,1,0:T(8,128)(2,1)S(1)} %bitcast.39), kind=kOutput, calls=%fused_computation.9 | convolution fusion | flops 67117056 | bytes 2621440 | tf_op jit(solution)/shard_map/anr,ars->ans/dot_general | solution.py:639
  147.5 0.0 copy-done
  147.5 0.0 copy-start.2
  147.5 2.8 %fusion.1 = f32[2,1,128,2048]{3,2,1,0:T(8,128)} fusion(f32[2,1,128,2048]{3,2,1,0:T(8,128)S(1)} %copy-done, bf16[2,2048,128]{2,1,0:T(8,128)(2,1)S(1)} %bitcast.40, bf16[2,2048,64]{1,2,0:T(8,128)(2,1)} %fusion.5, s32[]{:T(128)S(6)} %select_n.14), kind=kOutput, calls=%fused_computation.3 | convolution fusion | flops 67633152 | bytes 5275652 | tf_op jit(solution)/shard_map/ans,ams->anm/dot_general | solution.py:643
  150.4 0.0 copy-done.2
  150.4 0.6 copy.31
  (4 shorter events, 0.0 us)
Async XLA Ops:
  141.4 1.8 %copy-start.3 = (f32[8,2048]{1,0:T(8,128)S(1)}, f32[8,2048]{1,0:T(8,128)}, u32[]{:S(2)}) copy-start(f32[8,2048]{1,0:T(8,128)} %get-tuple-element.11) | copy-start | bytes 196612
  141.5 2.5 %copy-start.1 = (bf16[2,16,128,128]{3,2,1,0:T(8,128)(2,1)S(1)}, bf16[2,16,128,128]{3,2,1,0:T(8,128)(2,1)}, u32[]{:S(2)}) copy-start(bf16[2,16,128,128]{3,2,1,0:T(8,128)(2,1)} %get-tuple-element.9) | copy-start | bytes 3145732
  145.8 1.7 %copy-start = (f32[2,1,128,2048]{3,2,1,0:T(8,128)S(1)}, f32[2,1,128,2048]{3,2,1,0:T(8,128)}, u32[]{:S(2)}) copy-start(f32[2,1,128,2048]{3,2,1,0:T(8,128)} %tiles_ref.1) | copy-start | bytes 6291460
  147.5 2.8 %copy-start.2 = (f32[128,128]{1,0:T(8,128)S(1)}, f32[128,128]{1,0:T(8,128)}, u32[]{:S(2)}) copy-start(f32[128,128]{1,0:T(8,128)} %get-tuple-element.28) | copy-start | bytes 196612

commit v7 on v6

--- a/solution.py
+++ b/solution.py
@@ -101,11 +101,6 @@
     return first + lax.dot_general(lh, rl, NT, preferred_element_type=jnp.float32)
 
 
-def mul3(lh, ll, rh, rl):
-    def one(x, y):
-        return lax.dot_general(x, y, NT, preferred_element_type=jnp.float32)
-    return one(lh, rh) + (one(lh, rl) + one(ll, rh))
-
 MESH = pl.DeviceIdType.MESH
 
 
@@ -531,7 +526,7 @@
                 if s % 2 == 1 and s + 1 < count:
                     end = hi + 2 * BLK
                     for r0, r1 in spans(hi, 8 * BLK):
-                        work[r0:r1, :] = pair_given(r0, r1, s + 1) - mul3(
+                        work[r0:r1, :] = pair_given(r0, r1, s + 1) - mul2(
                             high[r0:r1, :hi], low[r0:r1, :hi],
                             high[hi:end, :hi], low[hi:end, :hi])
         return carry

time: 151 us -> 151 us (level)
  no operation moved by 1% of the time
where the time goes in v7:
time: 151 us
  Pallas kernels  135 us (89%)
  local copies, waits for them, and re-layouts  7.37 us (5%)
  matrix products  6.44 us (4%)
  other arithmetic  1.6 us (1%)
    pallas_call x1, Pallas kernels, update_call(): pl.pallas_call(update_kernel, out_shape=(jax.ShapeDtypeStruct((2, cols, B...  135 us
    unnamed x12, local copies, waits for them, and re-layouts  4.93 us

profile of v7, /device:TPU:1, one launch (start us, length us, event | category | flops | bytes accessed | tf_op | source)
XLA Modules:
  0.0 151.0 jit_solution(12254848957682694833)
XLA Ops:
  0.7 0.1 broadcast_compare_fusion
  0.8 1.3 copy.18.rank_ref
  2.0 0.8 and_select_fusion
  2.9 1.5 copy.19.left_ref
  4.4 1.5 copy.20.right_ref
  5.9 0.7 pad_convert_fusion.y_ref
  6.6 134.9 %shard_map.93 = (bf16[2,16,128,128]{3,2,1,0:T(8,128)(2,1)}, bf16[16,128,128]{2,1,0:T(8,128)(2,1)}, f32[8,2048]{1,0:T(8,128)}, f32[128,128]{1,0:T(8,128)}) custom-call(s32[2,1]{1,0:T(2,128)} %copy.18.rank_ref, bf16[2,1,128,64]{3,2,1,0:T(8,128)(2,1)} %copy.19.left_ref, bf16[2,1,128,64]{3,2,1,0:T(8,128)(2,1)} %copy.20.right_ref, f32[2,1,128,2048]{3,2,1,0:T(8,128)} %tiles_ref.1, ...), custom_call_target="tpu_custom_call" | custom-call | flops 99999997952 | bytes 20000000 | tf_op jit(solution)/shard_map/pallas_call | solution.py:567
  141.4 0.0 copy-start.3
  141.5 0.0 copy-start.1
  141.5 1.6 %copy.21 = bf16[16,128,128]{1,0,2:T(8,128)(2,1)S(1)} copy(bf16[16,128,128]{2,1,0:T(8,128)(2,1)} %get-tuple-element.8) | data formatting | bytes 1048576 | tf_op jit(solution)/shard_map/pallas_call | solution.py:567
  143.0 0.2 reshape.65
  143.3 0.0 copy-done.3
  143.3 0.7 reshape.64
  143.9 0.0 copy-done.1
  143.9 1.9 %fusion.3 = bf16[2,1,2,1,2048,64]{4,5,3,2,1,0:T(8,128)(2,1)} fusion(bf16[2048,2,64,1]{0,2,1,3:T(8,128)(2,1)S(1)} %reshape.65, pred[2,2]{1,0:T(4,128)(4,1)S(1)} %broadcast_compare_fusion, bf16[2,2048,128]{2,1,0:T(8,128)(2,1)S(1)} %bitcast.38), kind=kOutput, calls=%fused_computation.5 | convolution fusion | flops 135282688 | bytes 3670528 | tf_op jit(solution)/shard_map/anr,abrs->abns/dot_general | solution.py:648
  145.8 0.0 copy-start
  145.8 1.7 %fusion.5 = bf16[2,2048,64]{1,2,0:T(8,128)(2,1)} fusion(bf16[2,2048,128]{2,1,0:T(8,128)(2,1)S(1)} %bitcast.39), kind=kOutput, calls=%fused_computation.9 | convolution fusion | flops 67117056 | bytes 2621440 | tf_op jit(solution)/shard_map/anr,ars->ans/dot_general | solution.py:634
  147.5 0.0 copy-done
  147.5 0.0 copy-start.2
  147.5 2.8 %fusion.1 = f32[2,1,128,2048]{3,2,1,0:T(8,128)} fusion(f32[2,1,128,2048]{3,2,1,0:T(8,128)S(1)} %copy-done, bf16[2,2048,128]{2,1,0:T(8,128)(2,1)S(1)} %bitcast.40, bf16[2,2048,64]{1,2,0:T(8,128)(2,1)} %fusion.5, s32[]{:T(128)S(6)} %select_n.14), kind=kOutput, calls=%fused_computation.3 | convolution fusion | flops 67633152 | bytes 5275652 | tf_op jit(solution)/shard_map/ans,ams->anm/dot_general | solution.py:638
  150.4 0.0 copy-done.2
  150.4 0.6 copy.31
  (4 shorter events, 0.0 us)
Async XLA Ops:
  141.4 1.8 %copy-start.3 = (f32[8,2048]{1,0:T(8,128)S(1)}, f32[8,2048]{1,0:T(8,128)}, u32[]{:S(2)}) copy-start(f32[8,2048]{1,0:T(8,128)} %get-tuple-element.11) | copy-start | bytes 196612
  141.5 2.5 %copy-start.1 = (bf16[2,16,128,128]{3,2,1,0:T(8,128)(2,1)S(1)}, bf16[2,16,128,128]{3,2,1,0:T(8,128)(2,1)}, u32[]{:S(2)}) copy-start(bf16[2,16,128,128]{3,2,1,0:T(8,128)(2,1)} %get-tuple-element.9) | copy-start | bytes 3145732
  145.8 1.7 %copy-start = (f32[2,1,128,2048]{3,2,1,0:T(8,128)S(1)}, f32[2,1,128,2048]{3,2,1,0:T(8,128)}, u32[]{:S(2)}) copy-start(f32[2,1,128,2048]{3,2,1,0:T(8,128)} %tiles_ref.1) | copy-start | bytes 6291460
  147.5 2.8 %copy-start.2 = (f32[128,128]{1,0:T(8,128)S(1)}, f32[128,128]{1,0:T(8,128)}, u32[]{:S(2)}) copy-start(f32[128,128]{1,0:T(8,128)} %get-tuple-element.28) | copy-start | bytes 196612
